TPU v7x, 32 devices: a whole 2x2x4 slice. The times are simulated.
32 devices in a mesh: dp: 8 (over y, x, core), col: 4 (over z).
Axes of the slice: x: 2, y: 2, z: 4, core: 2. Of those that a mesh axis runs over, the one named last changes fastest.
Arguments:
- item_ids: int32 [256, 32], P('dp'), may hold values from 0 to 37482
- target_ids: int32 [256, 32], P('dp'), may hold values from 0 to 37482
- negative_ids: int32 [2048], replicated, may hold values from 0 to 37482
- reset_mask: int32 [256, 32], P('dp'), may hold values 0 or 1
- carry_flags: int32 [256], P('dp'), may hold values 0 or 1
- carried_state: float32 [256, 1000], P('dp', 'col'), may hold values from -3 to 3
- embed_table: float32 [1000, 37888], P('col'), may hold values from -6 to 6
- input_weight: float32 [3, 1000, 1000], P(None, 'col'), may hold values from -0.1875 to 0.1875
- hidden_weight: float32 [3, 1000, 1000], P(None, 'col'), may hold values from -0.1875 to 0.1875
- gate_bias: float32 [3, 1000], P(None, 'col'), may hold values from -3 to 3
- hidden_bias: float32 [1000], P('col'), may hold values from -3 to 3
- out_table: float32 [1000, 37888], P('col'), may hold values from -0.5 to 0.5
- out_bias: float32 [37888], replicated, may hold values from -3 to 3
Outputs:
- loss: float32 [256, 32], P('dp')
- grad_embed: float32 [1000, 37888], P('col', 'dp')
- grad_input_weight: float32 [3, 1000, 1000], P(None, 'col')
- grad_hidden_weight: float32 [3, 1000, 1000], P(None, 'col')
- grad_gate_bias: float32 [3, 1000], P(None, 'col')
- grad_hidden_bias: float32 [1000], P('col')
- grad_out_table: float32 [1000, 37888], P('col', 'dp')
- grad_out_bias: float32 [37888], P('dp')
- grad_carried: float32 [256, 1000], P('dp', 'col')
All inputs are finite; a program needn't handle non-finite values. No bound on the sum of `reset_mask` or of `carry_flags` on one device may be relied on, other than what follows from the above.
Results may differ from a plain program's by a relative error of at most 0.0003.
Values sent between devices are 32-bit elements; how exact they have to be, the bound alone decides.
A program may use at most 384 MiB of HBM per device.

v0:
```python
import jax
import jax.numpy as jnp
from jax import lax
from jax.sharding import PartitionSpec as P

bpr_weight = 1.0
precise = lax.Precision.HIGHEST


def combined_all(value, axis, join):
    pieces = jax.tree.map(lambda part: lax.all_gather(part, axis), value)
    head = jax.tree.map(lambda part: part[0], pieces)
    tail = jax.tree.map(lambda part: part[1:], pieces)
    subtotal, _ = lax.scan(lambda subtotal, section: (join(subtotal, section), None), head, tail)
    return subtotal


def gather_state(own_units):
    return lax.all_gather(own_units, "col", axis=1, tiled=True)


def scatter_state(partial_full):
    return lax.psum_scatter(partial_full, "col", scatter_dimension=1, tiled=True)


def combine_stats(first, second):
    top = jnp.maximum(first[0], second[0])
    scale_first = jnp.exp(first[0] - top)
    scale_second = jnp.exp(second[0] - top)
    return (
        top,
        first[1] * scale_first + second[1] * scale_second,
        first[2] * scale_first + second[2] * scale_second,
        first[3] * scale_first + second[3] * scale_second,
        first[4] * scale_first + second[4] * scale_second,
    )


def local(
    item_ids,
    target_ids,
    negative_ids,
    reset_mask,
    carry_flags,
    carried_state,
    embed_table,
    input_weight,
    hidden_weight,
    gate_bias,
    hidden_bias,
    out_table,
    out_bias,
):
    sessions, steps = item_ids.shape
    factor = 1.0 / steps
    items_time = item_ids.T
    targets_time = target_ids.T
    keep_time = (1 - reset_mask.T).astype(jnp.float32)
    flags = carry_flags.astype(jnp.float32)[:, None]
    embed_own = embed_table[:, items_time]
    inputs_full = lax.all_gather(embed_own, "col", axis=0, tiled=True)
    x_gates = jnp.einsum("dts,god->tsgo", inputs_full, input_weight, precision=precise) + gate_bias
    start_own = flags * carried_state
    start_full = gather_state(start_own)

    def forward_step(state, slices):
        own_state, full_state = state
        x_now, keep_now = slices
        prev_own = keep_now[:, None] * own_state
        prev_full = keep_now[:, None] * full_state
        h_gates = jnp.einsum("sk,gok->sgo", prev_full, hidden_weight, precision=precise)
        reset_gate = jax.nn.sigmoid(x_now[:, 0] + h_gates[:, 0])
        update_gate = jax.nn.sigmoid(x_now[:, 1] + h_gates[:, 1])
        inner = h_gates[:, 2] + hidden_bias
        candidate = jnp.tanh(x_now[:, 2] + reset_gate * inner)
        new_own = (1.0 - update_gate) * candidate + update_gate * prev_own
        new_full = gather_state(new_own)
        return (
            (new_own, new_full),
            (prev_full, prev_own, reset_gate, update_gate, candidate, inner, new_own, new_full),
        )

    final_state, kept = lax.scan(forward_step, (start_own, start_full), (x_gates, keep_time))
    prev_fulls, prev_owns, resets, updates, candidates, inners, outs_own, outs_full = kept
    target_cols = out_table[:, targets_time]
    target_part = jnp.einsum("tsk,kts->ts", outs_own, target_cols)
    pos_score = lax.psum(target_part, "col") + out_bias[targets_time]
    neg_cols = lax.all_to_all(
        out_table[:, negative_ids], "col", split_axis=1, concat_axis=0, tiled=True
    )
    neg_count = neg_cols.shape[1]
    my_negs = lax.dynamic_slice_in_dim(negative_ids, lax.axis_index("col") * neg_count, neg_count)
    neg_score = (
        jnp.einsum("tsk,kn->tsn", outs_full, neg_cols, precision=precise) + out_bias[my_negs]
    )
    local_top = jnp.max(neg_score, axis=-1)
    expd = jnp.exp(neg_score - local_top[..., None])
    sig = jax.nn.sigmoid(pos_score[..., None] - neg_score)
    stats = (
        local_top,
        jnp.sum(expd, axis=-1),
        jnp.sum(expd * sig, axis=-1),
        jnp.sum(expd * sig * (1.0 - sig), axis=-1),
        jnp.sum(expd * neg_score * neg_score, axis=-1),
    )
    top, denom, sig_sum, slope_sum, square_sum = combined_all(stats, "col", combine_stats)
    ppos = sig_sum / denom
    quad = square_sum / denom
    loss = -jnp.log(ppos) + bpr_weight * quad
    soft = jnp.exp(neg_score - top[..., None]) / denom[..., None]
    grad_neg = (
        factor
        * soft
        * (
            1.0
            - sig * sig / ppos[..., None]
            + bpr_weight * (neg_score * neg_score + 2.0 * neg_score - quad[..., None])
        )
    )
    grad_pos = -factor * (slope_sum / denom) / ppos
    neg_partial = jnp.einsum("tsn,kn->tsk", grad_neg, neg_cols, precision=precise)
    neg_table_grad = jnp.einsum("tsn,tsk->kn", grad_neg, outs_full, precision=precise)
    neg_back = lax.all_to_all(neg_table_grad, "col", split_axis=0, concat_axis=1, tiled=True)
    neg_bias_all = lax.all_gather(jnp.sum(grad_neg, axis=(0, 1)), "col", axis=0, tiled=True)
    target_state_grad = grad_pos[..., None] * jnp.moveaxis(target_cols, 0, -1)
    loss_grads = (
        lax.psum_scatter(neg_partial, "col", scatter_dimension=2, tiled=True) + target_state_grad
    )

    def backward_step(carry, slices):
        pending_part, pending_direct = carry
        (
            prev_full,
            prev_own,
            reset_gate,
            update_gate,
            candidate,
            inner,
            keep_now,
            loss_now,
            extra_now,
        ) = slices
        grad_state = scatter_state(pending_part) + pending_direct + loss_now
        grad_cand = grad_state * (1.0 - update_gate) * (1.0 - candidate * candidate)
        grad_reset = grad_cand * inner * reset_gate * (1.0 - reset_gate)
        grad_update = grad_state * (prev_own - candidate) * update_gate * (1.0 - update_gate)
        grad_inner = grad_cand * reset_gate
        dx_now = jnp.stack([grad_reset, grad_update, grad_cand], axis=1)
        dh_now = jnp.stack([grad_reset, grad_update, grad_inner], axis=1)
        partial_value = keep_now[:, None] * jnp.einsum(
            "sgo,gok->sk", dh_now, hidden_weight, precision=precise
        )
        direct = keep_now[:, None] * grad_state * update_gate
        return ((partial_value, direct), (dx_now, dh_now))

    zero_part = jnp.zeros(start_full.shape, jnp.float32)
    zero_own = jnp.zeros(start_own.shape, jnp.float32)
    last_carry, grads_time = lax.scan(
        backward_step,
        (zero_part, zero_own),
        (prev_fulls, prev_owns, resets, updates, candidates, inners, keep_time, loss_grads, None),
        reverse=True,
    )
    dx_gates, dh_gates = grads_time
    grad_start = scatter_state(last_carry[0]) + last_carry[1]
    grad_carried = flags * grad_start
    local_input = jnp.einsum("dts,tsgo->god", inputs_full, dx_gates, precision=precise)
    local_hidden = jnp.einsum("tsk,tsgo->gok", prev_fulls, dh_gates, precision=precise)
    local_gate = jnp.sum(dx_gates, axis=(0, 1))
    local_hbias = jnp.sum(dh_gates[:, :, 2], axis=(0, 1))
    grad_input, grad_hidden, grad_gate, grad_hbias = lax.psum(
        (local_input, local_hidden, local_gate, local_hbias), "dp"
    )
    input_partial = jnp.einsum("tsgo,god->dts", dx_gates, input_weight, precision=precise)
    grad_inputs_own = lax.psum_scatter(input_partial, "col", scatter_dimension=0, tiled=True)
    target_table_grad = jnp.moveaxis(grad_pos[..., None] * outs_own, -1, 0)
    out_dense = jnp.zeros(out_table.shape, jnp.float32)
    out_dense = (
        out_dense.at[:, targets_time].add(target_table_grad).at[:, negative_ids].add(neg_back)
    )
    bias_dense = jnp.zeros(out_bias.shape, jnp.float32)
    bias_dense = bias_dense.at[targets_time].add(grad_pos).at[negative_ids].add(neg_bias_all)
    grad_out, grad_obias = (
        lax.psum_scatter(out_dense, "dp", scatter_dimension=1, tiled=True),
        lax.psum_scatter(bias_dense, "dp", scatter_dimension=0, tiled=True),
    )
    embed_dense = jnp.zeros(embed_table.shape, jnp.float32).at[:, items_time].add(grad_inputs_own)
    grad_embed = lax.psum_scatter(embed_dense, "dp", scatter_dimension=1, tiled=True)
    return (
        loss.T,
        grad_embed,
        grad_input,
        grad_hidden,
        grad_gate,
        grad_hbias,
        grad_out,
        grad_obias,
        grad_carried,
    )


def solution(mesh):
    in_specs = (
        P("dp", None),
        P("dp", None),
        P(),
        P("dp", None),
        P("dp"),
        P("dp", "col"),
        P("col", None),
        P(None, "col", None),
        P(None, "col", None),
        P(None, "col"),
        P("col"),
        P("col", None),
        P(),
    )
    out_specs = (
        P("dp", None),
        P("col", "dp"),
        P(None, "col", None),
        P(None, "col", None),
        P(None, "col"),
        P("col"),
        P("col", "dp"),
        P("dp"),
        P("dp", "col"),
    )
    return jax.shard_map(local, mesh=mesh, in_specs=in_specs, out_specs=out_specs, check_vma=False)
```

profile of v0, /device:TPU:13, one launch (start us, length us, event | category | flops | bytes accessed | tf_op | source)
XLA Modules:
  0.0 3624.6 jit_solution(5470674001622310466)
XLA Ops:
  8.3 38.6 %copy.86 = f32[250,37888]{0,1:T(8,128)} copy(f32[250,37888]{1,0:T(8,128)} %param.25) | data formatting | bytes 75776000 | tf_op args[6]
  68.3 39.3 %copy.90 = f32[250,37888]{0,1:T(8,128)} copy(f32[250,37888]{1,0:T(8,128)} %param.30) | data formatting | bytes 75776000 | tf_op args[11]
  163.0 92.7 %all-gather.7 = f32[4,250,32]{1,2,0:T(8,128)S(1)} all-gather(f32[1,250,32]{1,2,0:T(8,128)S(1)} %fusion.87), channel_id=1, replica_groups=mesh['dp'=8,'col'=4] {'col'}, dimensions={0}, use_global_device_ids=true | all-gather | bytes 160000 | tf_op jit(solution)/shard_map/all_gather | solution.py:19
  259.1 133.9 %all-gather.13.cloned.1.call-done = f32[1000,32,32]{2,1,0:T(8,128)} async-done(((f32[250,32,32]{2,1,0:T(8,128)}), f32[1000,32,32]{2,1,0:T(8,128)}) %all-gather.13.cloned.1.call-update) | async-done | bytes 4096016 | tf_op jit(solution)/shard_map/all_gather | solution.py:61
  418.3 587.0 %while.67 = (s32[]{:T(128)}, f32[32,250]{1,0:T(8,128)S(1)}, f32[32,1000]{1,0:T(8,128)S(1)}, f32[32,32,1000]{2,1,0:T(8,128)}, f32[32,32,250]{2,1,0:T(8,128)}, /*i...) while((s32[]{:T(128)}, f32[32,250]{1,0:T(8,128)S(1)}, ...), condition=%wide.region_1.2_spmd, body=%wide.region_0.1_spmd.sunk | while | flops 288264000 | bytes 5196509 | solution.py:83
  1099.8 259.4 %all-reduce.15.cloned.1.call-done = f32[32,32,1000]{2,1,0:T(8,128)} async-done(((f32[32,32,1000]{2,1,0:T(8,128)}), f32[32,32,1000]{2,1,0:T(8,128)}) %all-reduce.15.cloned.1.call-update) | async-done | bytes 4096016
  1367.3 1454.1 %while.69 = (s32[]{:T(128)}, f32[32,1000]{1,0:T(8,128)S(1)}, f32[32,250]{1,0:T(8,128)S(1)}, f32[32,32,3,250]{3,1,2,0:T(8,128)}, f32[32,32,3,250]{3,1,2,0:T(8,128...) while((s32[]{:T(128)}, f32[32,1000]{1,0:T(8,128)S(1)}, ...), condition=%wide.region_13.14_spmd.clone, body=%wide.region_11.13_spmd.clone.sunk | while | flops 288368000 | bytes 5155580 | solution.py:158
  1549.9 35.8 all-reduce.21.cloned.1.call-done
  1595.5 35.9 all-reduce.21.cloned.1.call-done
  1641.2 35.8 all-reduce.21.cloned.1.call-done
  1732.1 35.8 all-reduce.21.cloned.1.call-done
  1823.0 35.8 all-reduce.21.cloned.1.call-done
  2186.1 35.8 all-reduce.21.cloned.1.call-done
  2231.8 35.9 all-reduce.21.cloned.1.call-done
  2277.4 35.8 all-reduce.21.cloned.1.call-done
  2368.3 35.8 all-reduce.21.cloned.1.call-done
  2550.2 35.9 all-reduce.21.cloned.1.call-done
  2641.2 35.8 all-reduce.21.cloned.1.call-done
  2686.8 35.8 all-reduce.21.cloned.1.call-done
  2777.7 35.9 all-reduce.21.cloned.1.call-done
  2902.6 96.3 %all_to_all.38 = f32[4,250,512]{2,1,0:T(8,128)} all-to-all(f32[4,250,512]{2,1,0:T(8,128)S(1)} %all_to_all.32), channel_id=1, replica_groups=mesh['dp'=8,'col'=4] {'col'}, dimensions={0} | all-to-all | bytes 4096000 | tf_op jit(solution)/shard_map/all_to_all | solution.py:123
  3022.9 37.3 %scatter_fusion = f32[250,37888]{0,1:T(8,128)} fusion(f32[250,37888]{0,1:T(8,128)} %scatter_custom_fusion.1, s32[2048]{0:T(1024)S(1)} %get-tuple-element.624, f32[2048,250]{1,0:T(8,128)S(1)} %bitcast.302), kind=kCustom, calls=%fused_computation.7 | custom fusion | flops 512000 | bytes 6152192 | tf_op jit(solution)/shard_map/scatter-add | solution.py:179
  3142.0 230.6 %reduce-scatter.9.cloned.1.call-done = f32[250,4736]{0,1:T(8,128)} async-done(((f32[250,37888]{0,1:T(8,128)}), f32[250,4736]{0,1:T(8,128)}) %reduce-scatter.9.cloned.1.call-update) | async-done | bytes 4736016 | tf_op jit(solution)/shard_map/reduce_scatter | solution.py:184
  3378.3 228.0 %reduce-scatter.7.cloned.1.call-done = f32[250,4736]{0,1:T(8,128)} async-done(((f32[250,37888]{0,1:T(8,128)}), f32[250,4736]{0,1:T(8,128)}) %reduce-scatter.7.cloned.1.call-update) | async-done | bytes 4736016 | tf_op jit(solution)/shard_map/reduce_scatter | solution.py:188
  (821 shorter events, 1964.0 us)
Async XLA Ops:
  7.2 385.8 %all-gather.13.cloned.1.call-start = ((), (), s32[]{:S(2)}) async-start(), calls=%async_computation.6 | async-start | bytes 20480000 | tf_op jit(solution)/shard_map/all_gather | solution.py:61
  131.2 124.7 %all-to-all-start = ((f32[250,4,512]{2,0,1:T(8,128)}), f32[250,4,512]{2,0,1:T(8,128)}, u32[]{:S(2)}, u32[]{:S(2)}) async-start(f32[250,4,512]{2,0,1:T(8,128)} %copy.91), calls=%async_computation | async-start | bytes 4194304 | tf_op jit(solution)/shard_map/all_to_all | solution.py:88
  136.2 1223.0 %all-reduce.15.cloned.1.call-start = ((), (), s32[]{:S(2)}) async-start(), calls=%async_computation.7 | async-start | bytes 8388608
  1547.9 37.8 %all-reduce.21.cloned.1.call-start = ((), (), s32[]{:S(2)}) async-start(), calls=%async_computation.10 | async-start | bytes 262144 | tf_op jit(solution)/shard_map/while
  1593.5 37.9 %all-reduce.21.cloned.1.call-start = ((), (), s32[]{:S(2)}) async-start(), calls=%async_computation.10 | async-start | bytes 262144 | tf_op jit(solution)/shard_map/while
  1639.2 37.8 %all-reduce.21.cloned.1.call-start = ((), (), s32[]{:S(2)}) async-start(), calls=%async_computation.10 | async-start | bytes 262144 | tf_op jit(solution)/shard_map/while
  1730.1 37.8 %all-reduce.21.cloned.1.call-start = ((), (), s32[]{:S(2)}) async-start(), calls=%async_computation.10 | async-start | bytes 262144 | tf_op jit(solution)/shard_map/while
  1821.0 37.8 %all-reduce.21.cloned.1.call-start = ((), (), s32[]{:S(2)}) async-start(), calls=%async_computation.10 | async-start | bytes 262144 | tf_op jit(solution)/shard_map/while
  1957.3 37.5 %all-reduce.21.cloned.1.call-start = ((), (), s32[]{:S(2)}) async-start(), calls=%async_computation.10 | async-start | bytes 262144 | tf_op jit(solution)/shard_map/while
  2002.6 37.5 %all-reduce.21.cloned.1.call-start = ((), (), s32[]{:S(2)}) async-start(), calls=%async_computation.10 | async-start | bytes 262144 | tf_op jit(solution)/shard_map/while
  2093.2 37.8 %all-reduce.21.cloned.1.call-start = ((), (), s32[]{:S(2)}) async-start(), calls=%async_computation.10 | async-start | bytes 262144 | tf_op jit(solution)/shard_map/while
  2184.1 37.8 %all-reduce.21.cloned.1.call-start = ((), (), s32[]{:S(2)}) async-start(), calls=%async_computation.10 | async-start | bytes 262144 | tf_op jit(solution)/shard_map/while
  2229.8 37.9 %all-reduce.21.cloned.1.call-start = ((), (), s32[]{:S(2)}) async-start(), calls=%async_computation.10 | async-start | bytes 262144 | tf_op jit(solution)/shard_map/while
  2275.4 37.8 %all-reduce.21.cloned.1.call-start = ((), (), s32[]{:S(2)}) async-start(), calls=%async_computation.10 | async-start | bytes 262144 | tf_op jit(solution)/shard_map/while
  2366.3 37.8 %all-reduce.21.cloned.1.call-start = ((), (), s32[]{:S(2)}) async-start(), calls=%async_computation.10 | async-start | bytes 262144 | tf_op jit(solution)/shard_map/while
  2502.6 37.8 %all-reduce.21.cloned.1.call-start = ((), (), s32[]{:S(2)}) async-start(), calls=%async_computation.10 | async-start | bytes 262144 | tf_op jit(solution)/shard_map/while
  2548.2 37.9 %all-reduce.21.cloned.1.call-start = ((), (), s32[]{:S(2)}) async-start(), calls=%async_computation.10 | async-start | bytes 262144 | tf_op jit(solution)/shard_map/while
  2639.2 37.8 %all-reduce.21.cloned.1.call-start = ((), (), s32[]{:S(2)}) async-start(), calls=%async_computation.10 | async-start | bytes 262144 | tf_op jit(solution)/shard_map/while
  2684.8 37.8 %all-reduce.21.cloned.1.call-start = ((), (), s32[]{:S(2)}) async-start(), calls=%async_computation.10 | async-start | bytes 262144 | tf_op jit(solution)/shard_map/while
  2775.7 37.9 %all-reduce.21.cloned.1.call-start = ((), (), s32[]{:S(2)}) async-start(), calls=%async_computation.10 | async-start | bytes 262144 | tf_op jit(solution)/shard_map/while
  2821.4 238.9 %all-reduce.19.cloned.1.call-start = ((), (), s32[]{:S(2)}) async-start(), calls=%async_computation.9 | async-start | bytes 8650752
  2834.7 304.3 %all-reduce.17.cloned.1.call-start = ((), (), s32[]{:S(2)}) async-start(), calls=%async_computation.8 | async-start | bytes 12591104 | tf_op jit(solution)/shard_map/psum | solution.py:171
  2889.6 483.0 %reduce-scatter.9.cloned.1.call-start = ((), (), s32[]{:S(2)}) async-start(), calls=%async_computation.5 | async-start | bytes 43646976 | tf_op jit(solution)/shard_map/reduce_scatter | solution.py:184
  3060.2 546.1 %reduce-scatter.7.cloned.1.call-start = ((), (), s32[]{:S(2)}) async-start(), calls=%async_computation.4 | async-start | bytes 43646976 | tf_op jit(solution)/shard_map/reduce_scatter | solution.py:188
  (37 other events, 1211.6 us)
Sparse Core Ops, SparseCore 0:
  68.4 324.5 all-gather.12
  1098.0 261.1 all-reduce.14
  1506.0 34.0 all-reduce.20
  1597.2 34.0 all-reduce.20
  1642.9 34.0 all-reduce.20
  1733.8 34.0 all-reduce.20
  1824.7 34.0 all-reduce.20
  1870.0 34.0 all-reduce.20
  1960.7 34.0 all-reduce.20
  2006.0 34.0 all-reduce.20
  2051.3 34.0 all-reduce.20
  2187.9 34.0 all-reduce.20
  2233.5 34.0 all-reduce.20
  2324.4 34.0 all-reduce.20
  2460.7 34.0 all-reduce.20
  2551.9 34.0 all-reduce.20
  2597.3 34.0 all-reduce.20
  2642.9 34.0 all-reduce.20
  2688.5 34.0 all-reduce.20
  2779.4 34.0 all-reduce.20
  2834.8 192.5 all-reduce.18
  3032.0 107.0 all-reduce.16
  3142.6 230.0 reduce-scatter.8
  3376.3 229.9 reduce-scatter.6
  (14 shorter events, 475.3 us)
where the time goes:
time: 3640 us; the launch traced here: 3620 us
  waiting for transfers between devices  2020 us (55%)
  blocking collectives  623 us (17%)
  matrix products  349 us (10%)
  other arithmetic  310 us (9%)
  local copies, waits for them, and re-layouts  275 us (8%)
    while x64, waiting for transfers between devices  1140 us
    all_gather x33, blocking collectives, gather_state(): return lax.all_gather(own_units, 'col', axis=1, tiled=True)  434 us
    unnamed x8, waiting for transfers between devices  260 us
    reduce_scatter x1, waiting for transfers between devices, local(): lax.psum_scatter(out_dense, 'dp', scatter_dimension=1, tiled=True)  231 us
    reduce_scatter x1, waiting for transfers between devices, local(): lax.psum_scatter(embed_dense, 'dp', scatter_dimension=1, tiled=True)  228 us
    dot_general x32, matrix products, backward_step(): jnp.einsum('sgo,gok->sk', dh_now, hidden_weight, precision=precise)  145 us
    all_gather x1, waiting for transfers between devices, local(): inputs_full = lax.all_gather(embed_own, 'col', axis=0, tiled=True)  134 us
    dot_general x32, matrix products, forward_step(): jnp.einsum('sk,gok->sgo', prev_full, hidden_weight, precision=precise)  120 us
  transfers between devices with their start and end apart: 39, of which 37 were waited for; matrix products, arithmetic and copies ran while one was open for 7% of the time, Pallas kernels for 0%

commit v1 on v0

v1 whole, which is shorter than its diff:
```python
import functools

import jax
import jax.numpy as jnp
from jax import lax
from jax.experimental import pallas as pl
from jax.experimental.pallas import tpu as pltpu
from jax.sharding import PartitionSpec as P

LANES = 128
ROWS8 = 8
VMEM_BYTES = 60 << 20
f32 = jnp.float32
bf16 = jnp.bfloat16
high = lax.Precision.HIGH


def round_up(value, unit):
    return -(-value // unit) * unit


def params():
    return pltpu.CompilerParams(vmem_limit_bytes=VMEM_BYTES)


def in_vmem():
    return pl.BlockSpec(memory_space=pltpu.VMEM)


def in_smem():
    return pl.BlockSpec(memory_space=pltpu.SMEM)


def gather_kernel(chunk, count, width, ids, table, bias, out, padded, turned):
    step = pl.program_id(0)

    @pl.when(step == 0)
    def _():
        padded[...] = jnp.zeros_like(padded)

    padded[0:width, :] = table[...]
    padded[width : width + 1, :] = bias[...]
    turned[pl.ds(pl.multiple_of(step * chunk, chunk), chunk), :] = padded[...].T

    @pl.when(step == pl.num_programs(0) - 1)
    def _():
        def body(block, carry):
            for j in range(ROWS8):
                row = ids[block * ROWS8 + j]
                out[pl.ds(block * ROWS8 + j, 1), :] = turned[pl.ds(row, 1), :]
            return carry

        lax.fori_loop(0, count // ROWS8, body, 0)


def gather_rows(table, bias, ids, block):
    width, rows = table.shape
    count = ids.shape[0]
    chunk = LANES * max(k for k in range(1, 9) if rows % (LANES * k) == 0)
    return pl.pallas_call(
        functools.partial(gather_kernel, chunk, count, width),
        out_shape=jax.ShapeDtypeStruct((count, block), f32),
        grid_spec=pltpu.PrefetchScalarGridSpec(
            num_scalar_prefetch=1,
            grid=(rows // chunk,),
            in_specs=[
                pl.BlockSpec((width, chunk), lambda i, ids: (0, i)),
                pl.BlockSpec((1, chunk), lambda i, ids: (0, i)),
            ],
            out_specs=pl.BlockSpec((count, block), lambda i, ids: (0, 0)),
            scratch_shapes=[pltpu.VMEM((block, chunk), f32), pltpu.VMEM((rows, block), f32)],
        ),
        compiler_params=params(),
    )(ids, table, bias)


def scatter_kernel(width, n_lists, *refs):
    bounds = refs[0]
    lists = refs[1 : 1 + 3 * n_lists]
    out, bias_out, acc = refs[1 + 3 * n_lists :]
    acc[...] = jnp.zeros_like(acc)
    low = bounds[0]
    for k in range(n_lists):
        rows_of, ids, data = lists[3 * k : 3 * k + 3]

        def body(i, carry):
            spot = pl.ds(ids[i] - low, 1)
            acc[spot, :] = acc[spot, :] + data[pl.ds(rows_of[i], 1), :]
            return carry

        lax.fori_loop(bounds[1 + 2 * k], bounds[2 + 2 * k], body, 0)
    for j in range(acc.shape[0] // LANES):
        cols = slice(j * LANES, (j + 1) * LANES)
        turned = acc[cols, :].T
        out[:, cols] = turned[:width]
        bias_out[:, cols] = turned[width : width + 1]


def scatter_rows(lists, low, own_rows, width, block):
    ends = [low]
    operands, specs = [], []
    for order, ids, data in lists:
        ends += [jnp.sum(ids < low, dtype=jnp.int32), jnp.sum(ids < low + own_rows, dtype=jnp.int32)]
        operands += [order, ids, data]
        specs += [in_smem(), in_smem(), in_vmem()]
    return pl.pallas_call(
        functools.partial(scatter_kernel, width, len(lists)),
        out_shape=(
            jax.ShapeDtypeStruct((width, own_rows), f32),
            jax.ShapeDtypeStruct((1, own_rows), f32),
        ),
        in_specs=[in_smem()] + specs,
        out_specs=(in_vmem(), in_vmem()),
        scratch_shapes=[pltpu.VMEM((own_rows, block), f32)],
        compiler_params=params(),
    )(jnp.stack(ends), *operands)


def split_weight(weight, high_part, low_part):
    step = 128

    @pl.loop(0, weight.shape[0] // step)
    def _(i):
        rows = pl.ds(pl.multiple_of(i * step, step), step)
        value = weight[rows, :]
        top = value.astype(bf16)
        high_part[rows, :] = top
        low_part[rows, :] = (value - top.astype(f32)).astype(bf16)


def two_part(value):
    top = value.astype(bf16).astype(f32)
    return jnp.concatenate([top, value - top], axis=0).astype(bf16)


def forward_kernel(
    steps, width, weight, x_gates, keep, start, prevs, resets, updates, cands, inners, outs, w_high, w_low
):
    rows_per, units = start.shape
    split_weight(weight, w_high, w_low)
    lane = lax.broadcasted_iota(jnp.int32, (rows_per, units), 1)

    def step(t, state):
        rows = pl.ds(pl.multiple_of(t * rows_per, rows_per), rows_per)
        prev = jnp.where(lane == width, 1.0, keep[rows, :] * state)
        pair = two_part(prev)

        def gate(g):
            cols = slice(g * units, (g + 1) * units)
            first = jnp.dot(pair, w_high[:, cols], preferred_element_type=f32)
            second = jnp.dot(pair, w_low[:, cols], preferred_element_type=f32)
            return first[:rows_per] + first[rows_per:] + second[:rows_per], cols

        h_reset, cols = gate(0)
        reset = jax.nn.sigmoid(x_gates[rows, cols] + h_reset)
        h_update, cols = gate(1)
        update = jax.nn.sigmoid(x_gates[rows, cols] + h_update)
        inner, cols = gate(2)
        cand = jnp.tanh(x_gates[rows, cols] + reset * inner)
        new = (1.0 - update) * cand + update * prev
        prevs[rows, :] = prev
        resets[rows, :] = reset
        updates[rows, :] = update
        cands[rows, :] = cand
        inners[rows, :] = inner
        outs[rows, :] = new
        return new

    lax.fori_loop(0, steps, step, start[...])


def run_forward(weight_turned, x_gates, keep, start, steps, width):
    events, units = x_gates.shape[0], start.shape[1]
    saved = jax.ShapeDtypeStruct((events, units), f32)
    return pl.pallas_call(
        functools.partial(forward_kernel, steps, width),
        out_shape=(saved,) * 6,
        in_specs=[in_vmem()] * 4,
        out_specs=(in_vmem(),) * 6,
        scratch_shapes=[pltpu.VMEM(weight_turned.shape, bf16)] * 2,
        compiler_params=params(),
    )(weight_turned, x_gates, keep, start)


def backward_kernel(
    steps, weight, douts, keep, prevs, resets, updates, cands, inners, dgates, dstart, w_high, w_low
):
    rows_per, units = dstart.shape
    split_weight(weight, w_high, w_low)

    def step(i, dstate):
        t = steps - 1 - i
        rows = pl.ds(pl.multiple_of(t * rows_per, rows_per), rows_per)
        reset, update, cand = resets[rows, :], updates[rows, :], cands[rows, :]
        dh = douts[rows, :] + dstate
        dcand = dh * (1.0 - update) * (1.0 - cand * cand)
        dreset = dcand * inners[rows, :] * reset * (1.0 - reset)
        dupdate = dh * (prevs[rows, :] - cand) * update * (1.0 - update)
        dinner = dcand * reset
        dgates[rows, 0:units] = dreset
        dgates[rows, units : 2 * units] = dupdate
        dgates[rows, 2 * units : 3 * units] = dinner
        dgates[rows, 3 * units : 4 * units] = dcand
        total = dh * update
        for g, part in enumerate((dreset, dupdate, dinner)):
            pair = two_part(part)
            sect = slice(g * units, (g + 1) * units)
            first = jnp.dot(pair, w_high[sect, :], preferred_element_type=f32)
            second = jnp.dot(pair, w_low[sect, :], preferred_element_type=f32)
            total = total + (first[:rows_per] + first[rows_per:] + second[:rows_per])
        return keep[rows, :] * total

    dstart[...] = lax.fori_loop(0, steps, step, jnp.zeros((rows_per, units), f32))


def run_backward(weight, douts, keep, saved, rows_per, steps):
    events, units = douts.shape
    return pl.pallas_call(
        functools.partial(backward_kernel, steps),
        out_shape=(
            jax.ShapeDtypeStruct((events, 4 * units), f32),
            jax.ShapeDtypeStruct((rows_per, units), f32),
        ),
        in_specs=[in_vmem()] * 8,
        out_specs=(in_vmem(),) * 2,
        scratch_shapes=[pltpu.VMEM(weight.shape, bf16)] * 2,
        compiler_params=params(),
    )(weight, douts, keep, *saved)


def pad_units(weight, bias, n_col, block):
    gates, own, full = weight.shape
    part = full // n_col
    rows = weight.reshape(gates, own, n_col, part)
    rows = jnp.pad(rows, ((0, 0), (0, block - own), (0, 0), (0, block - part)))
    rows = rows.reshape(gates, block, n_col * block)
    return rows.at[:, :own, part].set(bias)


def gather_weight(own, n_dp):
    gates, block, units = own.shape
    flat = own.reshape(n_dp, gates * block // n_dp, units)
    piece = lax.dynamic_index_in_dim(flat, lax.axis_index("dp"), 0, keepdims=False)
    every = lax.all_gather(piece, ("col", "dp"))
    every = every.reshape(-1, gates, block, units)
    return jnp.moveaxis(every, 0, 1).reshape(gates, -1, units)


def reduce_weight(partial, n_dp, n_col):
    gates, rows, units = partial.shape
    block = rows // n_col
    parts = jnp.moveaxis(partial.reshape(gates, n_col, block, units), 1, 0)
    parts = jnp.moveaxis(parts.reshape(n_col, n_dp, gates * block // n_dp, units), 1, 0)
    mine = lax.psum_scatter(parts, "dp", scatter_dimension=0)
    mine = lax.psum_scatter(mine, "col", scatter_dimension=0)
    return lax.all_gather(mine, "dp").reshape(gates, block, units)


def swap_col(rows, n_col):
    return lax.all_to_all(rows, "col", split_axis=0, concat_axis=0, tiled=True)


def unpad_last(value, n_col, part):
    block = value.shape[-1] // n_col
    return value.reshape(value.shape[:-1] + (n_col, block))[..., :part].reshape(value.shape[:-1] + (n_col * part,))


def local(
    n_dp,
    n_col,
    item_ids,
    target_ids,
    negative_ids,
    reset_mask,
    carry_flags,
    carried_state,
    embed_table,
    input_weight,
    hidden_weight,
    gate_bias,
    hidden_bias,
    out_table,
    out_bias,
):
    sessions, steps = item_ids.shape
    own_sessions = sessions // n_col
    rows_per = round_up(own_sessions, ROWS8)
    width = embed_table.shape[0]
    table_rows = embed_table.shape[1]
    own_rows = table_rows // n_dp
    block = round_up(width + 1, LANES)
    units = n_col * block
    events = steps * rows_per
    factor = 1.0 / steps
    dp_at, col_at = lax.axis_index("dp"), lax.axis_index("col")

    def by_owner(value):
        value = jnp.moveaxis(value.reshape(n_col, own_sessions, steps), 1, 2)
        value = jnp.pad(value, ((0, 0), (0, 0), (0, rows_per - own_sessions)))
        return value.reshape(-1)

    item_flat, target_flat = by_owner(item_ids), by_owner(target_ids)
    own_keep = lax.dynamic_index_in_dim(
        by_owner(1 - reset_mask).reshape(n_col, events, 1), col_at, 0, keepdims=False
    ).astype(f32)
    valid = jnp.tile(jnp.arange(rows_per) < own_sessions, steps)
    lane = jnp.arange(units) % block
    first_pad = jnp.arange(units) == width

    own_in = pad_units(input_weight, gate_bias, n_col, block)
    no_bias = jnp.zeros_like(hidden_bias)
    own_hid = pad_units(hidden_weight, jnp.stack([no_bias, no_bias, hidden_bias]), n_col, block)
    all_hid = gather_weight(own_hid, n_dp).reshape(-1, units)
    all_in = gather_weight(own_in, n_dp).reshape(-1, units)

    all_items = lax.all_gather(item_flat, "dp", tiled=True)
    all_targets = lax.all_gather(target_flat, "dp", tiled=True)

    def ordered(ids):
        ids, order = lax.sort((ids, lax.iota(jnp.int32, ids.shape[0])), num_keys=1)
        return order, ids

    no_row = jnp.zeros((1, table_rows), f32)
    item_rows = gather_rows(embed_table, no_row, item_flat, block).reshape(n_col, events, block)
    carried = (carry_flags.astype(f32)[:, None] * carried_state).reshape(n_col, own_sessions, width)
    carried = jnp.pad(carried, ((0, 0), (0, rows_per - own_sessions), (0, block - width)))
    arrived = swap_col(jnp.concatenate([item_rows, carried], axis=1), n_col)
    arrived = jnp.moveaxis(arrived, 0, 1).reshape(events + rows_per, units)
    inputs = jnp.where(first_pad, 1.0, arrived[:events])
    start = arrived[events:]

    neg_count = negative_ids.shape[0]
    own_negs = lax.dynamic_slice_in_dim(negative_ids, dp_at * (neg_count // n_dp), neg_count // n_dp)
    out_rows = gather_rows(out_table, out_bias[None, :], jnp.concatenate([target_flat, own_negs]), block)
    targets = swap_col(out_rows[: n_col * events].reshape(n_col, events, block), n_col)
    targets = jnp.moveaxis(targets, 0, 1).reshape(events, units)
    negs = lax.all_gather(out_rows[n_col * events :], ("dp", "col")).reshape(n_dp, n_col, -1, block)
    negs = jnp.moveaxis(negs, 1, 2).reshape(neg_count, units)

    x_gates = lax.dot_general(inputs, all_in, (((1,), (1,)), ((), ())), precision=high)
    prevs, resets, updates, cands, inners, outs = run_forward(
        all_hid.T, x_gates, own_keep, start, steps, width
    )

    shares = jnp.where(lane == width, 1.0 / n_col, jnp.where(lane < width, outs, 0.0))
    pos_score = jnp.sum(shares * targets, axis=-1, keepdims=True)
    neg_score = lax.dot_general(shares, negs, (((1,), (1,)), ((), ())), precision=high)
    top = jnp.max(neg_score, axis=-1, keepdims=True)
    expd = jnp.exp(neg_score - top)
    weight = expd / jnp.sum(expd, axis=-1, keepdims=True)
    sig = jax.nn.sigmoid(pos_score - neg_score)
    ppos = jnp.sum(weight * sig, axis=-1, keepdims=True)
    quad = jnp.sum(weight * neg_score * neg_score, axis=-1, keepdims=True)
    slope = jnp.sum(weight * sig * (1.0 - sig), axis=-1, keepdims=True)
    own_loss = (-jnp.log(ppos) + quad).reshape(steps, rows_per)[:, :own_sessions]
    loss = lax.all_gather(own_loss.T, "col", tiled=True)
    dneg = factor * weight * (1.0 - sig * sig / ppos + neg_score * neg_score + 2.0 * neg_score - quad)
    dneg = jnp.where(valid[:, None], dneg, 0.0)
    dpos = jnp.where(valid[:, None], -factor * slope / ppos, 0.0)
    douts = jnp.dot(dneg, negs, precision=high) + dpos * targets
    douts = jnp.where(lane < width, douts, 0.0)
    neg_part = lax.dot_general(dneg, shares, (((0,), (0,)), ((), ())), precision=high)
    target_part = dpos * shares

    neg_own = lax.psum_scatter(neg_part.reshape(n_dp, -1, units), "dp", scatter_dimension=0)
    neg_own = jnp.moveaxis(neg_own.reshape(-1, n_col, block), 1, 0)
    neg_own = lax.psum_scatter(neg_own, "col", scatter_dimension=0)
    neg_all = lax.all_gather(neg_own, "dp", tiled=True)
    target_own = swap_col(jnp.moveaxis(target_part.reshape(events, n_col, block), 1, 0), n_col)
    target_all = lax.all_gather(target_own.reshape(-1, block), "dp", tiled=True)
    low = (dp_at * own_rows).astype(jnp.int32)
    grad_out, grad_obias = scatter_rows(
        [ordered(all_targets) + (target_all,), ordered(negative_ids) + (neg_all,)],
        low,
        own_rows,
        width,
        block,
    )
    grad_obias = grad_obias[0] * n_col

    dgates, dstart = run_backward(
        all_hid, douts, own_keep, (prevs, resets, updates, cands, inners), rows_per, steps
    )
    dx = jnp.concatenate([dgates[:, : 2 * units], dgates[:, 3 * units :]], axis=1)
    dh = dgates[:, : 3 * units]
    hid_part = lax.dot_general(dh, prevs, (((0,), (0,)), ((), ())), precision=high)
    in_part = lax.dot_general(dx, inputs, (((0,), (0,)), ((), ())), precision=high)
    dinputs = jnp.dot(dx, all_in, precision=high)
    gates = input_weight.shape[0]
    back = jnp.concatenate([dinputs, dstart], axis=0).reshape(events + rows_per, n_col, block)
    back = swap_col(jnp.moveaxis(back, 1, 0), n_col)
    grad_carried = carry_flags.astype(f32)[:, None] * back[:, events : events + own_sessions, :width].reshape(
        sessions, width
    )
    item_all = lax.all_gather(back[:, :events].reshape(-1, block), "dp", tiled=True)
    grad_embed, _ = scatter_rows([ordered(all_items) + (item_all,)], low, own_rows, width, block)
    grad_in = reduce_weight(in_part.reshape(gates, units, units), n_dp, n_col)
    grad_hid = reduce_weight(hid_part.reshape(gates, units, units), n_dp, n_col)
    grad_in, grad_hid = grad_in[:, :width], grad_hid[:, :width]
    return (
        loss,
        grad_embed,
        unpad_last(grad_in, n_col, width),
        unpad_last(grad_hid, n_col, width),
        grad_in[:, :, width],
        grad_hid[gates - 1, :, width],
        grad_out,
        grad_obias,
        grad_carried,
    )


def solution(mesh):
    in_specs = (
        P("dp", None),
        P("dp", None),
        P(),
        P("dp", None),
        P("dp"),
        P("dp", "col"),
        P("col", None),
        P(None, "col", None),
        P(None, "col", None),
        P(None, "col"),
        P("col"),
        P("col", None),
        P(),
    )
    out_specs = (
        P("dp", None),
        P("col", "dp"),
        P(None, "col", None),
        P(None, "col", None),
        P(None, "col"),
        P("col"),
        P("col", "dp"),
        P("dp"),
        P("dp", "col"),
    )
    body = functools.partial(local, mesh.shape["dp"], mesh.shape["col"])
    return jax.shard_map(body, mesh=mesh, in_specs=in_specs, out_specs=out_specs, check_vma=False)
```

time: 3640 us -> 1280 us (0.35)
  waiting for transfers between devices: 2020 us -> 615 us
  blocking collectives: 623 us -> 118 us
  matrix products: 349 us -> 61.4 us
  other arithmetic: 310 us -> 35.4 us
  Pallas kernels: 0 us -> 246 us
  local copies, waits for them, and re-layouts: 275 us -> 164 us
    while x64 -> x0, waiting for transfers between devices: 1140 us -> none
    all_gather x39 -> x3, blocking collectives: 495 us -> 26.3 us  [the longest x1 9.22 us: local(): all_items = lax.all_gather(item_flat, 'dp', tiled=True)]
    reduce_scatter x2 -> x4, waiting for transfers between devices: 459 us -> 14.3 us  [the longest x2 14.2 us: reduce_weight(): mine = lax.psum_scatter(mine, 'col', scatter_dimension=0)]
    dot_general x71 -> x7, matrix products: 349 us -> 61.4 us  [the longest x1 9.98 us: local(): lax.dot_general(inputs, all_in, (((1,), (1,)), ((), ())), precision=high)]
    pallas_call x0 -> x6, Pallas kernels: none -> 246 us  [the longest x2 74 us: gather_rows(): pl.pallas_call(functools.partial(gather_kernel, chunk, count, width), out...]
    all_gather x1 -> x8, waiting for transfers between devices: 134 us -> 271 us  [the longest x2 153 us: gather_weight(): every = lax.all_gather(piece, ('col', 'dp'))]
    scatter-add x5 -> x0, other arithmetic: 99.4 us -> none  [the longest x2 59.3 us: local(): out_dense.at[:, targets_time].add(target_table_grad).at[:, negative_ids]]
    dynamic_update_slice x128 -> x0, other arithmetic: 90.4 us -> none  [the longest x96 67.7 us: local(): lax.scan(forward_step, (start_own, start_full), (x_gates, keep_time))]
  transfers between devices with their start and end apart: 39 -> 15, of which waited for: 37 -> 10; matrix products, arithmetic and copies ran while one was open for 7% -> 15% of each run, Pallas kernels for 0% -> 11%
where the time goes in v1:
time: 1280 us; the launch traced here: 1270 us
  waiting for transfers between devices  615 us (48%)
  Pallas kernels  246 us (19%)
  local copies, waits for them, and re-layouts  164 us (13%)
  blocking collectives  118 us (9%)
  matrix products  61.4 us (5%)
  other arithmetic  35.4 us (3%)
  between operations  14.6 us (1%)
    unnamed x14, waiting for transfers between devices  305 us
    all_gather x2, waiting for transfers between devices, gather_weight(): every = lax.all_gather(piece, ('col', 'dp'))  153 us
    all_to_all x2, blocking collectives, swap_col(): return lax.all_to_all(rows, 'col', split_axis=0, concat_axis=0, tiled=True)  91.7 us
    pallas_call x2, Pallas kernels, gather_rows(): pl.pallas_call(functools.partial(gather_kernel, chunk, count, width), out...  74 us
    pallas_call x1, Pallas kernels, run_forward(): pl.pallas_call(functools.partial(forward_kernel, steps, width), out_shape...  67.1 us
    pallas_call x1, Pallas kernels, run_backward(): pl.pallas_call(functools.partial(backward_kernel, steps), out_shape=(jax....  66.4 us
    all_gather x2, waiting for transfers between devices, reduce_weight(): return lax.all_gather(mine, 'dp').reshape(gates, block, units)  46.6 us
    pallas_call x2, Pallas kernels, scatter_rows(): pl.pallas_call(functools.partial(scatter_kernel, width, len(lists)), out_...  38.1 us
  transfers between devices with their start and end apart: 15, of which 10 were waited for; matrix products, arithmetic and copies ran while one was open for 15% of the time, Pallas kernels for 11%

profile of v1, /device:TPU:13, one launch (start us, length us, event | category | flops | bytes accessed | tf_op | source)
XLA Modules:
  0.0 1266.2 jit_solution(3752214205594927193)
XLA Ops:
  9.5 37.3 %shard_map.198 = f32[1280,256]{1,0:T(8,128)} custom-call(s32[1280]{0:T(1024)} %pad_add_fusion.ids, f32[250,37888]{1,0:T(8,128)} %table.3, f32[1,37888]{1,0:T(1,128)} %bitcast.186), custom_call_target="tpu_custom_call" | custom-call | tf_op jit(solution)/shard_map/pallas_call | solution.py:60
  85.9 36.6 %shard_map.196 = f32[1024,256]{1,0:T(8,128)} custom-call(s32[1024]{0:T(1024)} %reshape.267.ids, f32[250,37888]{1,0:T(8,128)} %table.2, f32[1,37888]{1,0:T(1,128)} %broadcast_in_dim.65.bias), custom_call_target="tpu_custom_call" | custom-call | tf_op jit(solution)/shard_map/pallas_call | solution.py:60
  132.7 25.0 %all-to-all-done = f32[4,264,256]{2,1,0:T(8,128)S(1)} async-done(((f32[4,264,256]{2,1,0:T(8,128)}), f32[4,264,256]{2,1,0:T(8,128)S(1)}, u32[]{:S(2)}, u32[]{:S(2)}) %all-to-all-start) | async-done | bytes 1081376 | tf_op jit(solution)/shard_map/all_to_all | solution.py:260
  158.6 10.5 copy.92
  169.1 10.7 copy.120
  179.8 67.1 %all-gather.13.cloned.1.call-done = f32[32,96,1024]{2,1,0:T(8,128)} async-done(((f32[1,96,1024]{2,1,0:T(8,128)}), f32[32,96,1024]{2,1,0:T(8,128)}) %all-gather.13.cloned.1.call-update) | async-done | bytes 12582928 | tf_op jit(solution)/shard_map/all_gather | solution.py:244
  246.9 11.9 copy.87
  258.8 85.8 %all-gather.11.cloned.1.call-done = f32[32,96,1024]{2,1,0:T(8,128)} async-done(((f32[1,96,1024]{2,1,0:T(8,128)}), f32[32,96,1024]{2,1,0:T(8,128)}) %all-gather.11.cloned.1.call-update) | async-done | bytes 12582928 | tf_op jit(solution)/shard_map/all_gather | solution.py:244
  344.6 11.8 copy.82
  356.4 12.7 %copy.89.weight = f32[1024,3072]{1,0:T(8,128)} copy(f32[1024,3072]{0,1:T(8,128)} %bitcast.138) | data formatting | bytes 25165824 | tf_op jit(solution)/shard_map/transpose | solution.py:342
  379.0 67.1 %shard_map.197 = (f32[256,1024]{1,0:T(8,128)}, f32[256,1024]{1,0:T(8,128)}, f32[256,1024]{1,0:T(8,128)}, f32[256,1024]{1,0:T(8,128)}, f32[256,1024]{1,0:T(8,128)}, /*index=5*/f32[256,1024]{1,0:T(8,128)}) custom-call(f32[1024,3072]{1,0:T(8,128)} %copy.89.weight, f32[256,3072]{1,0:T(8,128)} %fusion.37.x_gates, f32[256,1]{1,0:T(8,128)} %copy.90.keep, ...), custom_call_target="tpu_custom_call" | custom-call | tf_op jit(solution)/shard_map/pallas_call | solution.py:175
  486.6 66.4 %shard_map.199 = (f32[256,4096]{1,0:T(8,128)}, f32[8,1024]{1,0:T(8,128)}) custom-call(f32[3072,1024]{1,0:T(8,128)} %bitcast.139, f32[256,1024]{1,0:T(8,128)} %fusion.7.douts, f32[256,1]{1,0:T(8,128)} %copy.90.keep, f32[256,1024]{1,0:T(8,128)} %get-tuple-element.53.prevs, f32[256,1024]{1,0:T(8,128)} %get-tuple-element.54.resets, ...), custom_call_target="tpu_custom_call" | custom-call | tf_op jit(solution)/shard_map/pallas_call | solution.py:218
  571.2 11.9 copy.100
  592.3 11.8 copy.98
  607.3 303.5 %all-reduce.9.cloned.1.call-done = (f32[8,4,96,1024]{3,2,0,1:T(8,128)}, f32[8,4,96,1024]{3,2,0,1:T(8,128)}) async-done(((f32[8,4,96,1024]{3,2,0,1:T(8,128)}, f32[8,4,96,1024]{3,2,0,1:T(8,128)}), (f32[8,4,96,1024]{3,2,0,1:T(8,128)}, f32[8,4,96,1024]{3,2,0,1:T(8,128)})) %all-reduce.9.cloned.1.call-update) | async-done | bytes 25165840
  927.1 48.9 %all_to_all.20 = f32[4,264,256]{2,1,0:T(8,128)S(1)} all-to-all(f32[4,264,256]{2,1,0:T(8,128)S(1)} %bitcast.164), channel_id=1, replica_groups=mesh['dp'=8,'col'=4] {'col'}, dimensions={0} | all-to-all | bytes 2162688 | tf_op jit(solution)/shard_map/all_to_all | solution.py:260
  977.9 42.8 %all_to_all.21 = f32[4,256,256]{2,1,0:T(8,128)} all-to-all(f32[4,256,256]{2,1,0:T(8,128)S(1)} %bitcast.174), channel_id=1, replica_groups=mesh['dp'=8,'col'=4] {'col'}, dimensions={0} | all-to-all | bytes 2097152 | tf_op jit(solution)/shard_map/all_to_all | solution.py:260
  1022.1 14.2 %reduce-scatter.11.cloned.1.call-done = f32[1,96,1024]{2,1,0:T(8,128)} async-done(((f32[4,96,1024]{2,1,0:T(8,128)}), f32[1,96,1024]{2,1,0:T(8,128)}) %reduce-scatter.11.cloned.1.call-update) | async-done | bytes 393232 | tf_op jit(solution)/shard_map/reduce_scatter | solution.py:255
  1092.3 19.1 %shard_map.200 = (f32[250,4736]{1,0:T(8,128)}, f32[1,4736]{1,0:T(1,128)}) custom-call(s32[3]{0:T(128)} %pad_add_fusion.1.refs_0_, s32[8192]{0:T(1024)} %get-tuple-element.52.refs_1_, s32[8192]{0:T(1024)} %copy-done.10, f32[8192,256]{1,0:T(8,128)} %all-gather.15.cloned.1.call-done.refs_3_), custom_call_target="tpu_custom_call" | custom-call | tf_op jit(solution)/shard_map/pallas_call | solution.py:106
  1111.5 37.8 %all-gather.21.cloned.1.call-done.refs_3_ = f32[8192,256]{1,0:T(8,128)} async-done(((f32[1024,256]{1,0:T(8,128)}), f32[8192,256]{1,0:T(8,128)}) %all-gather.21.cloned.1.call-update) | async-done | bytes 8388624 | tf_op jit(solution)/shard_map/all_gather | solution.py:370
  1149.3 30.2 %all-gather.25.cloned.1.call-done = f32[1,2048,256]{2,1,0:T(8,128)} async-done(((f32[1,256,256]{2,1,0:T(8,128)}), f32[1,2048,256]{2,1,0:T(8,128)}) %all-gather.25.cloned.1.call-update) | async-done | bytes 2097168 | tf_op jit(solution)/shard_map/all_gather | solution.py:368
  1179.5 19.0 %shard_map.201 = (f32[250,4736]{1,0:T(8,128)}, f32[1,4736]{1,0:T(1,128)}) custom-call(s32[5]{0:T(128)} %stack.45.refs_0_, s32[8192]{0:T(1024)} %get-tuple-element.63.refs_1_, s32[8192]{0:T(1024)} %copy-done.9, f32[8192,256]{1,0:T(8,128)} %all-gather.21.cloned.1.call-done.refs_3_, s32[2048]{0:T(1024)} %get-tuple-element.64.refs_4_, s32[2048]{0:T(1024)} %copy-done.16, ...), custom_call_target="tpu_custom_call" | custom-call | tf_op jit(solution)/shard_map/pallas_call | solution.py:106
  1199.9 13.8 %all-gather.19.cloned.1.call-done = f32[8,96,1024]{2,1,0:T(8,128)} async-done(((f32[1,96,1024]{2,1,0:T(8,128)}), f32[8,96,1024]{2,1,0:T(8,128)}) %all-gather.19.cloned.1.call-update) | async-done | bytes 3145744 | tf_op jit(solution)/shard_map/all_gather | solution.py:256
  1215.4 32.7 %all-gather.17.cloned.1.call-done = f32[8,96,1024]{2,1,0:T(8,128)} async-done(((f32[1,96,1024]{2,1,0:T(8,128)}), f32[8,96,1024]{2,1,0:T(8,128)}) %all-gather.17.cloned.1.call-update) | async-done | bytes 3145744 | tf_op jit(solution)/shard_map/all_gather | solution.py:256
  (179 shorter events, 222.7 us)
Async XLA Ops:
  7.2 151.4 %all-gather.23.cloned.1.call-start = ((), (), s32[]{:S(2)}) async-start(), calls=%async_computation.18 | async-start | bytes 8650752 | tf_op jit(solution)/shard_map/all_gather | solution.py:337
  9.5 39.1 %copy-start.8 = (f32[3,250,1000]{1,2,0:T(8,128)S(1)}, f32[3,250,1000]{1,2,0:T(8,128)}, u32[]{:S(2)}) copy-start(f32[3,250,1000]{1,2,0:T(8,128)} %param.25) | copy-start | bytes 9000004
  48.5 198.3 %all-gather.13.cloned.1.call-start = ((), (), s32[]{:S(2)}) async-start(), calls=%async_computation.9 | async-start | bytes 12976128 | tf_op jit(solution)/shard_map/all_gather | solution.py:244
  69.5 275.0 %all-gather.11.cloned.1.call-start = ((), (), s32[]{:S(2)}) async-start(), calls=%async_computation.8 | async-start | bytes 12976128 | tf_op jit(solution)/shard_map/all_gather | solution.py:244
  79.6 45.3 %all-to-all-start.1 = ((f32[4,256,256]{2,1,0:T(8,128)}), f32[4,256,256]{2,1,0:T(8,128)S(1)}, u32[]{:S(2)}, u32[]{:S(2)}) async-start(f32[4,256,256]{2,1,0:T(8,128)} %bitcast.30), calls=%async_computation.1 | async-start | bytes 2097152 | tf_op jit(solution)/shard_map/all_to_all | solution.py:260
  85.9 36.6 %copy-start.15 = (f32[32,250]{1,0:T(8,128)S(1)}, f32[32,250]{1,0:T(8,128)}, u32[]{:S(2)}) copy-start(f32[32,250]{1,0:T(8,128)} %param.22) | copy-start | bytes 96004
  124.9 32.8 %all-to-all-start = ((f32[4,264,256]{2,1,0:T(8,128)}), f32[4,264,256]{2,1,0:T(8,128)S(1)}, u32[]{:S(2)}, u32[]{:S(2)}) async-start(f32[4,264,256]{2,1,0:T(8,128)} %select_maximum_fusion), calls=%async_computation | async-start | bytes 2162688 | tf_op jit(solution)/shard_map/all_to_all | solution.py:260
  131.2 472.9 %reduce-scatter.15.cloned.1.call-start = ((), (), s32[]{:S(2)}) async-start(), calls=%async_computation.16 | async-start | bytes 9437184 | tf_op jit(solution)/shard_map/reduce_scatter | solution.py:365
  132.7 313.5 %copy-start.6 = (f32[4,32,8,256]{3,2,0,1:T(8,128)}, f32[4,32,8,256]{3,2,0,1:T(8,128)S(1)}, u32[]{:S(2)}) copy-start(f32[4,32,8,256]{3,2,0,1:T(8,128)S(1)} %copy.119) | copy-start | bytes 3145732
  472.2 438.6 %all-reduce.9.cloned.1.call-start = ((), (), s32[]{:S(2)}) async-start(), calls=%async_computation.20 | async-start | bytes 50331648
  604.1 416.7 %reduce-scatter.17.cloned.1.call-start = ((), (), s32[]{:S(2)}) async-start(), calls=%async_computation.17 | async-start | bytes 1310720 | tf_op jit(solution)/shard_map/reduce_scatter | solution.py:367
  606.7 414.8 %reduce-scatter.13.cloned.1.call-start = ((), (), s32[]{:S(2)}) async-start(), calls=%async_computation.13 | async-start | bytes 1966080 | tf_op jit(solution)/shard_map/reduce_scatter | solution.py:255
  914.2 122.1 %reduce-scatter.11.cloned.1.call-start = ((), (), s32[]{:S(2)}) async-start(), calls=%async_computation.11 | async-start | bytes 1966080 | tf_op jit(solution)/shard_map/reduce_scatter | solution.py:255
  917.7 174.6 %all-gather.15.cloned.1.call-start = ((), (), s32[]{:S(2)}) async-start(), calls=%async_computation.10 | async-start | bytes 9437184 | tf_op jit(solution)/shard_map/all_gather | solution.py:395
  977.1 172.1 %all-gather.21.cloned.1.call-start = ((), (), s32[]{:S(2)}) async-start(), calls=%async_computation.15 | async-start | bytes 9437184 | tf_op jit(solution)/shard_map/all_gather | solution.py:370
  977.9 58.5 %copy-start.19 = (s32[2048]{0:T(1024)S(1)}, s32[2048]{0:T(1024)}, u32[]{:S(2)}) copy-start(s32[2048]{0:T(1024)} %param.19) | copy-start | bytes 24580
  977.9 63.5 %copy-start.11 = (s32[1024]{0:T(1024)S(1)}, s32[1024]{0:T(1024)}, u32[]{:S(2)}) copy-start(s32[1024]{0:T(1024)} %reshape.267.ids) | copy-start | bytes 12292
  977.9 79.5 %copy-start.13 = (s32[1024]{0:T(1024)S(1)}, s32[1024]{0:T(1024)}, u32[]{:S(2)}) copy-start(s32[1024]{0:T(1024)} %copy-done.12) | copy-start | bytes 12292
  1020.7 158.8 %all-gather.25.cloned.1.call-start = ((), (), s32[]{:S(2)}) async-start(), calls=%async_computation.19 | async-start | bytes 2359296 | tf_op jit(solution)/shard_map/all_gather | solution.py:368
  1021.5 192.3 %all-gather.19.cloned.1.call-start = ((), (), s32[]{:S(2)}) async-start(), calls=%async_computation.14 | async-start | bytes 3538944 | tf_op jit(solution)/shard_map/all_gather | solution.py:256
  1022.1 226.1 %all-gather.17.cloned.1.call-start = ((), (), s32[]{:S(2)}) async-start(), calls=%async_computation.12 | async-start | bytes 3538944 | tf_op jit(solution)/shard_map/all_gather | solution.py:256
  1041.4 70.1 %copy-start.16 = (s32[2048]{0:T(1024)}, s32[2048]{0:T(1024)S(1)}, u32[]{:S(2)}) copy-start(s32[2048]{0:T(1024)S(1)} %get-tuple-element.62.refs_5_) | copy-start | bytes 24580
  1057.4 34.9 %copy-start.10 = (s32[8192]{0:T(1024)}, s32[8192]{0:T(1024)S(1)}, u32[]{:S(2)}) copy-start(s32[8192]{0:T(1024)S(1)} %get-tuple-element.51.refs_2_) | copy-start | bytes 98308
  1072.6 38.9 %copy-start.9 = (s32[8192]{0:T(1024)}, s32[8192]{0:T(1024)S(1)}, u32[]{:S(2)}) copy-start(s32[8192]{0:T(1024)S(1)} %get-tuple-element.61.refs_2_) | copy-start | bytes 98308
  (16 other events, 76.5 us)
Sparse Core Ops, SparseCore 0:
  48.7 94.2 all-gather.22
  145.8 100.9 all-gather.12
  250.3 94.2 all-gather.10
  472.3 69.5 reduce-scatter.14
  604.2 306.6 all-reduce.8
  913.5 29.9 reduce-scatter.16
  946.5 47.0 reduce-scatter.12
  996.6 39.7 reduce-scatter.10
  1038.9 53.3 all-gather.14
  1094.2 55.0 all-gather.20
  1151.3 28.1 all-gather.24
  1181.4 32.2 all-gather.18
  1215.8 32.3 all-gather.16

commit v2 on v1

--- a/solution.py
+++ b/solution.py
@@ -13,6 +13,7 @@
 f32 = jnp.float32
 bf16 = jnp.bfloat16
 high = lax.Precision.HIGH
+MESH = pl.DeviceIdType.MESH
 
 
 def round_up(value, unit):
@@ -226,6 +227,399 @@
         scratch_shapes=[pltpu.VMEM(weight.shape, bf16)] * 2,
         compiler_params=params(),
     )(weight, douts, keep, *saved)
+
+
+def place():
+    d = lax.axis_index("dp")
+    c = lax.axis_index("col")
+    return d // 4, (d // 2) % 2, d % 2, c, d
+
+
+def greet(partners):
+    barrier = pltpu.get_barrier_semaphore()
+    for partner in partners:
+        pl.semaphore_signal(barrier, inc=1, device_id=partner, device_id_type=MESH)
+    pl.semaphore_wait(barrier, len(partners))
+
+
+def reduce_kernel(first, second, out, mine, core_in, x_in, y_in, xy_in, yx_in, z_in, total, local_sem, send_sem, recv_sem):
+    y, x, k, c, d = place()
+    half = mine.shape[4] // 2
+    core_to, x_to, y_to, far_to = ((d + 1 - 2 * k, c), (d + 2 - 4 * x, c), (d + 4 - 8 * y, c), (d + 6 - 4 * x - 8 * y, c))
+    z_to = [lax.rem(c + m, 4) for m in (1, 2, 3)]
+    greet([core_to, x_to, y_to, far_to] + [(d, z) for z in z_to])
+    partials = (first, second)
+    gates = first.shape[0]
+    jobs = 2 * gates
+
+    def send(j, slot, source, target, to):
+        copy = pltpu.make_async_remote_copy(
+            src_ref=source,
+            dst_ref=target,
+            send_sem=send_sem.at[j, slot],
+            recv_sem=recv_sem.at[j, slot],
+            device_id=to,
+            device_id_type=MESH,
+        )
+        copy.start()
+        return copy
+
+    started = [{} for _ in range(jobs)]
+    loads = []
+    for j in range(jobs):
+        source = partials[j // gates].at[j % gates]
+        load = pltpu.make_async_copy(source.at[:, :, :, k], mine.at[j], local_sem.at[j])
+        load.start()
+        loads.append(load)
+        started[j]["core"] = send(j, 0, source.at[:, :, :, 1 - k], core_in.at[j], core_to)
+
+    def stage_core(j):
+        loads[j].wait()
+        started[j]["core"].wait_recv()
+        for a in range(4):
+            for b in range(2):
+                for e in range(2):
+                    mine[j, a, b, e] = mine[j, a, b, e] + core_in[j, a, b, e]
+        started[j]["x"] = send(j, 1, mine.at[j, :, :, 1 - x, 0:half], x_in.at[j], x_to)
+        started[j]["y"] = send(j, 2, mine.at[j, :, 1 - y, :, half : 2 * half], y_in.at[j], y_to)
+
+    def stage_first(j):
+        started[j]["x"].wait_recv()
+        for a in range(4):
+            for b in range(2):
+                mine[j, a, b, x, 0:half] = mine[j, a, b, x, 0:half] + x_in[j, a, b]
+        started[j]["xy"] = send(j, 3, mine.at[j, :, 1 - y, x, 0:half], xy_in.at[j], y_to)
+        started[j]["y"].wait_recv()
+        for a in range(4):
+            for e in range(2):
+                mine[j, a, y, e, half : 2 * half] = mine[j, a, y, e, half : 2 * half] + y_in[j, a, e]
+        started[j]["yx"] = send(j, 4, mine.at[j, :, y, 1 - x, half : 2 * half], yx_in.at[j], x_to)
+
+    def stage_second(j):
+        started[j]["xy"].wait_recv()
+        started[j]["yx"].wait_recv()
+        for a in range(4):
+            mine[j, a, y, x, 0:half] = mine[j, a, y, x, 0:half] + xy_in[j, a]
+            mine[j, a, y, x, half : 2 * half] = mine[j, a, y, x, half : 2 * half] + yx_in[j, a]
+        for m in range(3):
+            started[j]["z", m] = send(j, 5 + m, mine.at[j, z_to[m], y, x], z_in.at[j, m], (d, z_to[m]))
+
+    def stage_z(j):
+        for m in range(3):
+            started[j]["z", m].wait_recv()
+        total[j] = ((mine[j, c, y, x] + z_in[j, 0]) + z_in[j, 1]) + z_in[j, 2]
+        spot = out.at[j // gates, j % gates, d]
+        keep = pltpu.make_async_copy(total.at[j], spot, local_sem.at[j])
+        keep.start()
+        started[j]["keep"] = keep
+        for slot, (name, to) in enumerate((("gx", x_to), ("gy", y_to), ("gf", far_to), ("gc", core_to))):
+            started[j][name] = send(j, 8 + slot, total.at[j], spot, to)
+
+    def stage_share(j):
+        for slot, (name, to) in enumerate((("gx", x_to), ("gy", y_to), ("gf", far_to))):
+            started[j][name].wait_recv()
+            spot = out.at[j // gates, j % gates, to[0]]
+            started[j]["c" + name] = send(j, 12 + slot, spot, spot, core_to)
+
+    def stage_end(j):
+        for name in ("gc", "cgx", "cgy", "cgf"):
+            started[j][name].wait_recv()
+        for name, copy in started[j].items():
+            if name == "keep":
+                copy.wait()
+            else:
+                copy.wait_send()
+
+    stages = (stage_core, stage_first, stage_second, stage_z, stage_share, stage_end)
+    for tick in range(jobs + len(stages) - 1):
+        for depth, stage in enumerate(stages):
+            if 0 <= tick - depth < jobs:
+                stage(tick - depth)
+
+
+def reduce_weights(first, second, collective_id):
+    gates, units, _ = first.shape
+    piece = units // 32
+    shape = (gates, 4, 2, 2, 2, piece, units)
+    jobs = 2 * gates
+    half = piece // 2
+    return pl.pallas_call(
+        reduce_kernel,
+        out_shape=jax.ShapeDtypeStruct((2, gates, 8, piece, units), f32),
+        in_specs=[pl.BlockSpec(memory_space=pl.ANY)] * 2,
+        out_specs=pl.BlockSpec(memory_space=pl.ANY),
+        scratch_shapes=[
+            pltpu.VMEM((jobs, 4, 2, 2, piece, units), f32),
+            pltpu.VMEM((jobs, 4, 2, 2, piece, units), f32),
+            pltpu.VMEM((jobs, 4, 2, half, units), f32),
+            pltpu.VMEM((jobs, 4, 2, half, units), f32),
+            pltpu.VMEM((jobs, 4, half, units), f32),
+            pltpu.VMEM((jobs, 4, half, units), f32),
+            pltpu.VMEM((jobs, 3, piece, units), f32),
+            pltpu.VMEM((jobs, piece, units), f32),
+            pltpu.SemaphoreType.DMA((jobs,)),
+            pltpu.SemaphoreType.DMA((jobs, 15)),
+            pltpu.SemaphoreType.DMA((jobs, 15)),
+        ],
+        compiler_params=pltpu.CompilerParams(
+            collective_id=collective_id, has_side_effects=True, vmem_limit_bytes=VMEM_BYTES
+        ),
+    )(first.reshape(shape), second.reshape(shape)).reshape(2, gates, 8 * piece, units)
+
+
+UNITS = ((0, 0), (0, 1), (1, 0), (0, 2), (1, 1), (1, 2))
+
+
+def head_kernel(
+    chunk,
+    width,
+    item_ids,
+    out_ids,
+    embed,
+    table,
+    bias,
+    own_in,
+    own_hid,
+    carried,
+    all_in,
+    all_hid,
+    arrived,
+    out_rows,
+    padded,
+    turned,
+    item_rows,
+    held,
+    local_sem,
+    send_sem,
+    recv_sem,
+    row_send,
+    row_recv,
+):
+    y, x, k, c, d = place()
+    i = pl.program_id(0)
+    n = pl.num_programs(0) // 2
+    core_to, x_to, y_to = (d + 1 - 2 * k, c), (d + 2 - 4 * x, c), (d + 4 - 8 * y, c)
+    z_all = (c + 1 - 2 * lax.rem(c, 2), lax.rem(c + 2, 4), 3 - c)
+    owns, alls = (own_in, own_hid), (all_in, all_hid)
+    piece = own_in.shape[4]
+    half = piece // 2
+    block = item_rows.shape[2]
+    items = item_rows.shape[1]
+    carried_rows = carried.shape[1]
+    events = items - carried_rows
+
+    def send(u, slot):
+        w, m = UNITS[u]
+        z = z_all[m]
+        every = alls[w]
+        if slot == 0:
+            source, target, to = owns[w].at[:, y, x, k], every.at[:, c, y, x, k], (d, z)
+        elif slot in (4, 6):
+            spot = (
+                every.at[:, z, y, 1 - x, k, 0:half] if slot == 4 else every.at[:, z, 1 - y, x, k, half : 2 * half]
+            )
+            source, target, to = spot, spot, (y_to if slot == 4 else x_to)
+        else:
+            py, px, to = {
+                1: (y, x, x_to),
+                2: (y, x, y_to),
+                3: (y, x, core_to),
+                5: (y, 1 - x, core_to),
+                7: (1 - y, x, core_to),
+                8: (1 - y, 1 - x, core_to),
+            }[slot]
+            spot = every.at[:, z, py, px, k]
+            source, target = spot, spot
+        return pltpu.make_async_remote_copy(
+            src_ref=source,
+            dst_ref=target,
+            send_sem=send_sem.at[u, slot],
+            recv_sem=recv_sem.at[u, slot],
+            device_id=to,
+            device_id_type=MESH,
+        )
+
+    def load(w):
+        return pltpu.make_async_copy(owns[w], held.at[w], local_sem.at[w])
+
+    def keep(w):
+        return pltpu.make_async_copy(held.at[w], alls[w].at[:, c], local_sem.at[2 + w])
+
+    def keep_own(_):
+        for w in range(2):
+            load(w).wait()
+            keep(w).start()
+
+    def item_send(m):
+        return pltpu.make_async_remote_copy(
+            src_ref=item_rows.at[z_all[m]],
+            dst_ref=arrived.at[:, pl.ds(pl.multiple_of(c * block, block), block)],
+            send_sem=row_send.at[m],
+            recv_sem=row_recv.at[m],
+            device_id=(d, z_all[m]),
+            device_id_type=MESH,
+        )
+
+    def begin_items(_):
+        for m in range(3):
+            item_send(m).start()
+
+    def item_keep():
+        return pltpu.make_async_copy(
+            item_rows.at[c], arrived.at[:, pl.ds(pl.multiple_of(c * block, block), block)], local_sem.at[4]
+        )
+
+    def begin():
+        greet([core_to, x_to, y_to] + [(d, z) for z in z_all])
+        begin_z(0)
+        begin_z(1)
+        load(0).start()
+        load(1).start()
+
+    def begin_z(u):
+        send(u, 0).start()
+
+    def spread(u):
+        send(u, 0).wait_recv()
+        for slot in (1, 2, 3):
+            send(u, slot).start()
+
+    def forward(u):
+        send(u, 1).wait_recv()
+        send(u, 4).start()
+        send(u, 5).start()
+        send(u, 2).wait_recv()
+        send(u, 6).start()
+        send(u, 7).start()
+
+    def far(u):
+        send(u, 4).wait_recv()
+        send(u, 6).wait_recv()
+        send(u, 8).start()
+
+    def close(u):
+        for slot in (3, 5, 7, 8):
+            send(u, slot).wait_recv()
+        for slot in range(9):
+            send(u, slot).wait_send()
+
+    timeline = [(-1, begin, None), (4, keep_own, 0), (64, begin_items, 0)]
+    timeline += [(at, begin_z, 2 + j) for j, at in enumerate((10, 18, 34, 50))]
+    for u, at in enumerate((11, 23, 34, 46, 58, 90)):
+        timeline += [(at, spread, u), (at + 12, forward, u), (at + 20, far, u)]
+    timeline.sort(key=lambda entry: entry[0])
+    last = 2 * n - 1
+
+    @pl.when(i == 0)
+    def _():
+        padded[...] = jnp.zeros_like(padded)
+
+    for at, action, u in timeline:
+        if at < last:
+
+            @pl.when(i == max(at, 0))
+            def _(action=action, u=u):
+                action() if u is None else action(u)
+
+    @pl.when(i < n)
+    def _():
+        padded[0:width, :] = embed[...]
+
+    @pl.when(i >= n)
+    def _():
+        padded[0:width, :] = table[...]
+        padded[width : width + 1, :] = bias[...]
+
+    spot = lax.rem(i, n) * chunk
+    turned[pl.ds(pl.multiple_of(spot, chunk), chunk), :] = padded[...].T
+
+    @pl.when(i == n - 1)
+    def _():
+        for z in range(4):
+
+            def body(b, carry, z=z):
+                for j in range(8):
+                    row = item_ids[z * events + b * 8 + j]
+                    item_rows[z, pl.ds(b * 8 + j, 1), :] = turned[pl.ds(row, 1), :]
+                return carry
+
+            lax.fori_loop(0, events // 8, body, 0)
+            item_rows[z, events:items, :] = carried[z]
+        item_keep().start()
+
+    @pl.when(i == last)
+    def _():
+        def body(b, carry):
+            for j in range(8):
+                row = out_ids[b * 8 + j]
+                out_rows[pl.ds(b * 8 + j, 1), :] = turned[pl.ds(row, 1), :]
+            return carry
+
+        lax.fori_loop(0, out_rows.shape[0] // 8, body, 0)
+        for at, action, u in timeline:
+            if at >= last:
+                action(u)
+        for u in range(6):
+            close(u)
+        for m in range(3):
+            item_send(m).wait()
+        for w in range(2):
+            keep(w).wait()
+        item_keep().wait()
+
+
+def gather_all(embed, table, bias, item_ids, out_ids, own_in, own_hid, carried, collective_id):
+    width, rows = embed.shape
+    gates, block, units = own_in.shape
+    piece = block // 8
+    chunk = 128 * max(k for k in range(1, 9) if rows % (128 * k) == 0)
+    n = rows // chunk
+    items = item_ids.shape[0] // 4 + carried.shape[1]
+    own_shape = (gates, 2, 2, 2, piece, units)
+    all_shape = (gates, 4, 2, 2, 2, piece, units)
+    smem = pl.BlockSpec(memory_space=pltpu.SMEM)
+    hbm = pl.BlockSpec(memory_space=pl.ANY)
+    all_in, all_hid, arrived, out_rows = pl.pallas_call(
+        functools.partial(head_kernel, chunk, width),
+        out_shape=(
+            jax.ShapeDtypeStruct(all_shape, f32),
+            jax.ShapeDtypeStruct(all_shape, f32),
+            jax.ShapeDtypeStruct((items, units), f32),
+            jax.ShapeDtypeStruct((out_ids.shape[0], block), f32),
+        ),
+        grid=(2 * n,),
+        in_specs=[
+            smem,
+            smem,
+            pl.BlockSpec((width, chunk), lambda i: (0, jnp.minimum(i, n - 1))),
+            pl.BlockSpec((width, chunk), lambda i: (0, jnp.maximum(i - n, 0))),
+            pl.BlockSpec((1, chunk), lambda i: (0, jnp.maximum(i - n, 0))),
+            hbm,
+            hbm,
+            pl.BlockSpec(carried.shape, lambda i: (0, 0, 0)),
+        ],
+        out_specs=(hbm, hbm, hbm, pl.BlockSpec((out_ids.shape[0], block), lambda i: (0, 0))),
+        scratch_shapes=[
+            pltpu.VMEM((block, chunk), f32),
+            pltpu.VMEM((rows, block), f32),
+            pltpu.VMEM((4, items, block), f32),
+            pltpu.VMEM((2,) + own_shape, f32),
+            pltpu.SemaphoreType.DMA((5,)),
+            pltpu.SemaphoreType.DMA((6, 9)),
+            pltpu.SemaphoreType.DMA((6, 9)),
+            pltpu.SemaphoreType.DMA((3,)),
+            pltpu.SemaphoreType.DMA((3,)),
+        ],
+        compiler_params=pltpu.CompilerParams(
+            collective_id=collective_id, has_side_effects=True, vmem_limit_bytes=VMEM_BYTES
+        ),
+    )(item_ids, out_ids, embed, table, bias, own_in.reshape(own_shape), own_hid.reshape(own_shape), carried)
+    return (
+        all_in.reshape(gates, 4 * block, units),
+        all_hid.reshape(gates, 4 * block, units),
+        arrived,
+        out_rows,
+    )
 
 
 def pad_units(weight, bias, n_col, block):
@@ -291,6 +685,7 @@
     block = round_up(width + 1, LANES)
     units = n_col * block
     events = steps * rows_per
+    direct = n_dp == 8 and n_col == 4 and block % 64 == 0
     factor = 1.0 / steps
     dp_at, col_at = lax.axis_index("dp"), lax.axis_index("col")
 
@@ -310,8 +705,6 @@
     own_in = pad_units(input_weight, gate_bias, n_col, block)
     no_bias = jnp.zeros_like(hidden_bias)
     own_hid = pad_units(hidden_weight, jnp.stack([no_bias, no_bias, hidden_bias]), n_col, block)
-    all_hid = gather_weight(own_hid, n_dp).reshape(-1, units)
-    all_in = gather_weight(own_in, n_dp).reshape(-1, units)
 
     all_items = lax.all_gather(item_flat, "dp", tiled=True)
     all_targets = lax.all_gather(target_flat, "dp", tiled=True)
@@ -320,18 +713,26 @@
         ids, order = lax.sort((ids, lax.iota(jnp.int32, ids.shape[0])), num_keys=1)
         return order, ids
 
-    no_row = jnp.zeros((1, table_rows), f32)
-    item_rows = gather_rows(embed_table, no_row, item_flat, block).reshape(n_col, events, block)
     carried = (carry_flags.astype(f32)[:, None] * carried_state).reshape(n_col, own_sessions, width)
     carried = jnp.pad(carried, ((0, 0), (0, rows_per - own_sessions), (0, block - width)))
-    arrived = swap_col(jnp.concatenate([item_rows, carried], axis=1), n_col)
-    arrived = jnp.moveaxis(arrived, 0, 1).reshape(events + rows_per, units)
+    neg_count = negative_ids.shape[0]
+    own_negs = lax.dynamic_slice_in_dim(negative_ids, dp_at * (neg_count // n_dp), neg_count // n_dp)
+    out_ids = jnp.concatenate([target_flat, own_negs])
+    if direct:
+        all_in, all_hid, arrived, out_rows = gather_all(
+            embed_table, out_table, out_bias[None, :], item_flat, out_ids, own_in, own_hid, carried, 1
+        )
+    else:
+        all_hid = gather_weight(own_hid, n_dp)
+        all_in = gather_weight(own_in, n_dp)
+        no_row = jnp.zeros((1, table_rows), f32)
+        item_rows = gather_rows(embed_table, no_row, item_flat, block).reshape(n_col, events, block)
+        arrived = swap_col(jnp.concatenate([item_rows, carried], axis=1), n_col)
+        arrived = jnp.moveaxis(arrived, 0, 1).reshape(events + rows_per, units)
+        out_rows = gather_rows(out_table, out_bias[None, :], out_ids, block)
+    all_hid, all_in = all_hid.reshape(-1, units), all_in.reshape(-1, units)
     inputs = jnp.where(first_pad, 1.0, arrived[:events])
     start = arrived[events:]
-
-    neg_count = negative_ids.shape[0]
-    own_negs = lax.dynamic_slice_in_dim(negative_ids, dp_at * (neg_count // n_dp), neg_count // n_dp)
-    out_rows = gather_rows(out_table, out_bias[None, :], jnp.concatenate([target_flat, own_negs]), block)
     targets = swap_col(out_rows[: n_col * events].reshape(n_col, events, block), n_col)
     targets = jnp.moveaxis(targets, 0, 1).reshape(events, units)
     negs = lax.all_gather(out_rows[n_col * events :], ("dp", "col")).reshape(n_dp, n_col, -1, block)
@@ -394,8 +795,13 @@
     )
     item_all = lax.all_gather(back[:, :events].reshape(-1, block), "dp", tiled=True)
     grad_embed, _ = scatter_rows([ordered(all_items) + (item_all,)], low, own_rows, width, block)
-    grad_in = reduce_weight(in_part.reshape(gates, units, units), n_dp, n_col)
-    grad_hid = reduce_weight(hid_part.reshape(gates, units, units), n_dp, n_col)
+    in_part, hid_part = in_part.reshape(gates, units, units), hid_part.reshape(gates, units, units)
+    if direct:
+        reduced = reduce_weights(in_part, hid_part, 2)
+        grad_in, grad_hid = reduced[0], reduced[1]
+    else:
+        grad_in = reduce_weight(in_part, n_dp, n_col)
+        grad_hid = reduce_weight(hid_part, n_dp, n_col)
     grad_in, grad_hid = grad_in[:, :width], grad_hid[:, :width]
     return (
         loss,

time: 1280 us -> 789 us (0.62)
  waiting for transfers between devices: 615 us -> 0.64 us
  Pallas kernels: 246 us -> 453 us
  local copies, waits for them, and re-layouts: 164 us -> 115 us
  blocking collectives: 118 us -> 95.4 us
    unnamed x14 -> x6, waiting for transfers between devices: 305 us -> 0.58 us
    all_gather x4 -> x0, waiting for transfers between devices: 199 us -> none  [the longest x2 153 us: gather_weight(): every = lax.all_gather(piece, ('col', 'dp'))]
    pallas_call x2, Pallas kernels: 74 us -> 273 us  [the longest x1 160 us: reduce_weights(): pl.pallas_call(reduce_kernel, out_shape=jax.ShapeDtypeStruct((2, gates, 8...]
    all_gather x1, waiting for transfers between devices: 37.8 us -> 0.01 us  [local(): target_all = lax.all_gather(target_own.reshape(-1, block), 'dp', tiled=True)]
    transpose x3 -> x0, local copies, waits for them, and re-layouts: 35.4 us -> none  [the longest x2 23.7 us: gather_weight(): return jnp.moveaxis(every, 0, 1).reshape(gates, -1, units)]
    all_gather x1, waiting for transfers between devices: 30.2 us -> 0.01 us  [local(): neg_all = lax.all_gather(neg_own, 'dp', tiled=True)]
    all_to_all x2 -> x1, waiting for transfers between devices: 25 us -> 0.01 us  [swap_col(): return lax.all_to_all(rows, 'col', split_axis=0, concat_axis=0, tiled=True)]
    all_to_all x2, blocking collectives: 91.7 us -> 67.1 us  [swap_col(): return lax.all_to_all(rows, 'col', split_axis=0, concat_axis=0, tiled=True)]
  transfers between devices with their start and end apart: 15 -> 7, of which waited for: 10 -> 0; matrix products, arithmetic and copies ran while one was open for 15% -> 15% of each run, Pallas kernels for 11% -> 41%
where the time goes in v2:
time: 789 us; the launch traced here: 779 us
  Pallas kernels  453 us (57%)
  local copies, waits for them, and re-layouts  115 us (15%)
  blocking collectives  95.4 us (12%)
  matrix products  57.9 us (7%)
  other arithmetic  31.5 us (4%)
  between operations  14.9 us (2%)
  starting transfers between devices  11.2 us (1%)
    pallas_call x1, Pallas kernels, reduce_weights(): pl.pallas_call(reduce_kernel, out_shape=jax.ShapeDtypeStruct((2, gates, 8...  160 us
    pallas_call x1, Pallas kernels, gather_all(): pl.pallas_call(functools.partial(head_kernel, chunk, width), out_shape=(j...  113 us
    pallas_call x1, Pallas kernels, run_backward(): pl.pallas_call(functools.partial(backward_kernel, steps), out_shape=(jax....  68.4 us
    all_to_all x2, blocking collectives, swap_col(): return lax.all_to_all(rows, 'col', split_axis=0, concat_axis=0, tiled=True)  67.1 us
    pallas_call x1, Pallas kernels, run_forward(): pl.pallas_call(functools.partial(forward_kernel, steps, width), out_shape...  66.7 us
    pallas_call x2, Pallas kernels, scatter_rows(): pl.pallas_call(functools.partial(scatter_kernel, width, len(lists)), out_...  44.6 us
    sort x3, other arithmetic, ordered(): ids, order = lax.sort((ids, lax.iota(jnp.int32, ids.shape[0])), num_keys=1)  18.6 us
  transfers between devices with their start and end apart: 7, of which 0 were waited for; matrix products, arithmetic and copies ran while one was open for 15% of the time, Pallas kernels for 41%

profile of v2, /device:TPU:13, one launch (start us, length us, event | category | flops | bytes accessed | tf_op | source)
XLA Modules:
  0.0 779.4 jit_solution(18259251962821856009)
XLA Ops:
  44.8 113.3 %shard_map.196 = (f32[3,4,2,2,2,32,1024]{6,5,4,3,2,1,0:T(8,128)}, f32[3,4,2,2,2,32,1024]{6,5,4,3,2,1,0:T(8,128)}, f32[264,1024]{1,0:T(8,128)}, f32[1280,256]{1,0:T(8,128)}) custom-call(s32[1024]{0:T(1024)} %reshape.229.item_ids, s32[1280]{0:T(1024)} %pad_add_fusion.out_ids, f32[250,37888]{1,0:T(8,128)} %embed.1, f32[250,37888]{1,0:T(8,128)} %table.1, ...), custom_call_target="tpu_custom_call" | custom-call | tf_op jit(solution)/shard_map/pallas_call | solution.py:582
  162.3 11.0 %all-to-all-start = ((f32[4,256,256]{2,1,0:T(8,128)}), f32[4,256,256]{2,1,0:T(8,128)}, u32[]{:S(2)}, u32[]{:S(2)}) async-start(f32[4,256,256]{2,1,0:T(8,128)} %bitcast.23), calls=%async_computation | async-start | bytes 2097152 | tf_op jit(solution)/shard_map/all_to_all | solution.py:654
  175.0 12.7 %copy.86.weight = f32[1024,3072]{1,0:T(8,128)} copy(f32[1024,3072]{0,1:T(8,128)} %bitcast.97) | data formatting | bytes 25165824 | tf_op jit(solution)/shard_map/transpose | solution.py:743
  187.7 10.0 %fusion.9.x_gates = f32[256,3072]{1,0:T(8,128)} fusion(f32[3072,1024]{1,0:T(8,128)} %bitcast.99, f32[264,1024]{1,0:T(8,128)S(1)} %copy-done.5, pred[1024]{0:T(1024)(128)(4,1)S(1)} %iota_compare_fusion), kind=kOutput, calls=%fused_computation.22 | convolution fusion | flops 4832100352 | bytes 16778240 | tf_op jit(solution)/shard_map/dot_general | solution.py:741
  197.7 66.7 %shard_map.197 = (f32[256,1024]{1,0:T(8,128)}, f32[256,1024]{1,0:T(8,128)}, f32[256,1024]{1,0:T(8,128)}, f32[256,1024]{1,0:T(8,128)}, f32[256,1024]{1,0:T(8,128)}, /*index=5*/f32[256,1024]{1,0:T(8,128)}) custom-call(f32[1024,3072]{1,0:T(8,128)} %copy.86.weight, f32[256,3072]{1,0:T(8,128)} %fusion.9.x_gates, f32[256,1]{1,0:T(8,128)} %copy.87.keep, ...), custom_call_target="tpu_custom_call" | custom-call | tf_op jit(solution)/shard_map/pallas_call | solution.py:176
  267.1 10.6 %copy.88 = f32[8,4,256,256]{2,0,3,1:T(8,128)} copy(f32[8,4,256,256]{3,2,1,0:T(8,128)} %bitcast.116) | data formatting | bytes 16777216 | tf_op jit(solution)/shard_map/reshape | solution.py:738
  277.7 7.5 copy.107
  291.6 7.5 fusion.10
  299.0 9.1 %copy.98 = f32[8,256,1024]{1,2,0:T(8,128)} copy(f32[8,256,1024]{2,1,0:T(8,128)} %bitcast.117) | data formatting | bytes 16777216 | tf_op jit(solution)/shard_map/reshape | solution.py:766
  309.4 9.1 %fusion.7.douts = f32[256,1024]{1,0:T(8,128)} fusion(f32[2048,1024]{0,1:T(8,128)} %bitcast.102, f32[256,1024]{1,0:T(8,128)S(1)} %bitcast.124, f32[256]{0:T(256)S(1)} %get-tuple-element.104, pred[1024]{0:T(1024)(128)(4,1)S(1)} %get-tuple-element.112, f32[256,2048]{1,0:T(8,128)S(1)} %get-tuple-element.109, f32[256]{0:T(256)S(1)} %get-tuple-element.94, ...), kind=kOutput, calls=%fused_computation.14 | convolution fusion | flops 3230924800 | bytes 12590336 | tf_op jit(solution)/shard_map/dot_general | solution.py:761
  318.5 68.4 %shard_map.198 = (f32[256,4096]{1,0:T(8,128)}, f32[8,1024]{1,0:T(8,128)}) custom-call(f32[3072,1024]{1,0:T(8,128)} %bitcast.98, f32[256,1024]{1,0:T(8,128)} %fusion.7.douts, f32[256,1]{1,0:T(8,128)} %copy.87.keep, f32[256,1024]{1,0:T(8,128)} %get-tuple-element.61.prevs, f32[256,1024]{1,0:T(8,128)} %get-tuple-element.62.resets, ...), custom_call_target="tpu_custom_call" | custom-call | tf_op jit(solution)/shard_map/pallas_call | solution.py:219
  392.6 9.1 %fusion.3 = f32[256,1024]{1,0:T(8,128)S(1)} fusion(f32[3072,1024]{1,0:T(8,128)} %bitcast.100, f32[256,1024]{1,0:T(8,128)S(1)} %slice.114, f32[256,2048]{1,0:T(8,128)S(1)} %slice.113), kind=kOutput, calls=%fused_computation.5 | convolution fusion | flops 4832624640 | bytes 16777216 | tf_op jit(solution)/shard_map/dot_general | solution.py:789
  401.9 39.1 %all_to_all.15 = f32[4,264,256]{2,1,0:T(8,128)S(1)} all-to-all(f32[4,264,256]{2,1,0:T(8,128)S(1)} %bitcast.119), channel_id=1, replica_groups=mesh['dp'=8,'col'=4] {'col'}, dimensions={0} | all-to-all | bytes 2162688 | tf_op jit(solution)/shard_map/all_to_all | solution.py:654
  444.7 28.0 %all_to_all.16 = f32[4,256,256]{2,1,0:T(8,128)} all-to-all(f32[4,256,256]{2,1,0:T(8,128)S(1)} %bitcast.126), channel_id=1, replica_groups=mesh['dp'=8,'col'=4] {'col'}, dimensions={0} | all-to-all | bytes 2097152 | tf_op jit(solution)/shard_map/all_to_all | solution.py:654
  478.3 10.4 %all_gather.27 = s32[8192]{0:T(1024)S(1)} all-gather(s32[1024]{0:T(1024)S(1)} %copy-done.11), channel_id=1, replica_groups=mesh['dp'=8,'col'=4] {'dp'}, dimensions={0}, use_global_device_ids=true | all-gather | bytes 36864 | tf_op jit(solution)/shard_map/all_gather | solution.py:709
  488.7 6.8 sort.45
  495.5 8.3 %all_gather.29 = s32[8192]{0:T(1024)S(1)} all-gather(s32[1024]{0:T(1024)S(1)} %reshape.231), channel_id=1, replica_groups=mesh['dp'=8,'col'=4] {'dp'}, dimensions={0}, use_global_device_ids=true | all-gather | bytes 36864 | tf_op jit(solution)/shard_map/all_gather | solution.py:710
  503.8 6.8 sort.46
  517.1 9.7 %all_gather.26 = f32[32,32]{1,0:T(8,128)S(1)} all-gather(f32[8,32]{1,0:T(8,128)S(1)} %copy.90), channel_id=1, replica_groups=mesh['dp'=8,'col'=4] {'col'}, dimensions={0}, use_global_device_ids=true | all-gather | bytes 5120 | tf_op jit(solution)/shard_map/all_gather | solution.py:757
  526.8 9.7 %fusion.2 = f32[3072,1024]{1,0:T(8,128)} fusion(f32[256,1024]{1,0:T(8,128)S(1)} %slice.114, f32[256,2048]{1,0:T(8,128)S(1)} %slice.113, f32[264,1024]{1,0:T(8,128)} %get-tuple-element.55, pred[1024]{0:T(1024)(128)(4,1)S(1)} %iota_compare_fusion), kind=kOutput, calls=%fused_computation.4 | convolution fusion | flops 4832886784 | bytes 16778240 | tf_op jit(solution)/shard_map/dot_general | solution.py:788
  536.5 8.1 %fusion = f32[3072,1024]{1,0:T(8,128)} fusion(f32[256,1024]{1,0:T(8,128)S(1)} %copy-done.8, f32[256,4096]{1,0:T(8,128)S(1)} %copy-done.2), kind=kOutput, calls=%fused_computation.1 | convolution fusion | flops 4831838208 | bytes 16777216 | tf_op jit(solution)/shard_map/dot_general | solution.py:787
  544.5 159.9 %shard_map.200 = f32[2,3,8,32,1024]{4,3,2,1,0:T(8,128)} custom-call(f32[3,4,2,2,2,32,1024]{6,5,4,3,2,1,0:T(8,128)} %bitcast.95, f32[3,4,2,2,2,32,1024]{6,5,4,3,2,1,0:T(8,128)} %bitcast.96), custom_call_target="tpu_custom_call" | custom-call | tf_op jit(solution)/shard_map/pallas_call | solution.py:346
  725.5 24.0 %shard_map.199 = (f32[250,4736]{1,0:T(8,128)}, f32[1,4736]{1,0:T(1,128)}) custom-call(s32[3]{0:T(128)} %pad_add_fusion.1.refs_0_, s32[8192]{0:T(1024)} %get-tuple-element.60.refs_1_, s32[8192]{0:T(1024)} %copy-done.10, f32[8192,256]{1,0:T(8,128)} %all-gather.7.cloned.1.call-done.refs_3_), custom_call_target="tpu_custom_call" | custom-call | tf_op jit(solution)/shard_map/pallas_call | solution.py:107
  749.6 20.6 %shard_map.201 = (f32[250,4736]{1,0:T(8,128)}, f32[1,4736]{1,0:T(1,128)}) custom-call(s32[5]{0:T(128)} %stack.45.refs_0_, s32[8192]{0:T(1024)} %get-tuple-element.71.refs_1_, s32[8192]{0:T(1024)} %copy-done.9, f32[8192,256]{1,0:T(8,128)} %all-gather.9.cloned.1.call-done.refs_3_, s32[2048]{0:T(1024)} %get-tuple-element.72.refs_4_, s32[2048]{0:T(1024)} %copy-done.14, ...), custom_call_target="tpu_custom_call" | custom-call | tf_op jit(solution)/shard_map/pallas_call | solution.py:107
  (137 shorter events, 98.2 us)
Async XLA Ops:
  7.2 259.9 %all-gather.11.cloned.1.call-start = ((), (), s32[]{:S(2)}) async-start(), calls=%async_computation.9 | async-start | bytes 8650752 | tf_op jit(solution)/shard_map/all_gather | solution.py:738
  7.9 6.5 copy-start.18
  10.9 3.5 copy-start.13
  27.0 3.6 copy-start.21
  27.0 6.4 copy-start.17
  27.0 7.3 copy-start.20
  27.0 8.1 %copy-start.16 = (s32[2048]{0:T(1024)S(1)}, s32[2048]{0:T(1024)}, u32[]{:S(2)}) copy-start(s32[2048]{0:T(1024)} %param.19) | copy-start | bytes 24580
  159.9 13.5 %copy-start.15 = (s32[32,32]{1,0:T(8,128)S(1)}, s32[32,32]{1,0:T(8,128)}, u32[]{:S(2)}) copy-start(s32[32,32]{1,0:T(8,128)} %param.20) | copy-start | bytes 12292
  159.9 14.5 %copy-start.5 = (f32[264,1024]{1,0:T(8,128)S(1)}, f32[264,1024]{1,0:T(8,128)}, u32[]{:S(2)}) copy-start(f32[264,1024]{1,0:T(8,128)} %get-tuple-element.55) | copy-start | bytes 3244036
  162.3 102.2 %all-to-all-start = ((f32[4,256,256]{2,1,0:T(8,128)}), f32[4,256,256]{2,1,0:T(8,128)}, u32[]{:S(2)}, u32[]{:S(2)}) async-start(f32[4,256,256]{2,1,0:T(8,128)} %bitcast.23), calls=%async_computation | async-start | bytes 2097152 | tf_op jit(solution)/shard_map/all_to_all | solution.py:654
  173.2 216.7 %reduce-scatter.3.cloned.1.call-start = ((), (), s32[]{:S(2)}) async-start(), calls=%async_computation.7 | async-start | bytes 9437184 | tf_op jit(solution)/shard_map/reduce_scatter | solution.py:766
  285.2 4.5 copy-start
  308.2 164.5 %reduce-scatter.5.cloned.1.call-start = ((), (), s32[]{:S(2)}) async-start(), calls=%async_computation.8 | async-start | bytes 1310720 | tf_op jit(solution)/shard_map/reduce_scatter | solution.py:768
  392.5 9.2 %copy-start.12 = (f32[8,1024]{1,0:T(8,128)S(1)}, f32[8,1024]{1,0:T(8,128)}, u32[]{:S(2)}) copy-start(f32[8,1024]{1,0:T(8,128)} %get-tuple-element.67) | copy-start | bytes 98308
  392.5 333.0 %all-gather.7.cloned.1.call-start = ((), (), s32[]{:S(2)}) async-start(), calls=%async_computation.5 | async-start | bytes 9437184 | tf_op jit(solution)/shard_map/all_gather | solution.py:796
  443.1 306.4 %all-gather.9.cloned.1.call-start = ((), (), s32[]{:S(2)}) async-start(), calls=%async_computation.6 | async-start | bytes 9437184 | tf_op jit(solution)/shard_map/all_gather | solution.py:771
  444.6 33.7 %copy-start.11 = (s32[1024]{0:T(1024)S(1)}, s32[1024]{0:T(1024)}, u32[]{:S(2)}) copy-start(s32[1024]{0:T(1024)} %reshape.229.item_ids) | copy-start | bytes 12292
  472.7 276.9 %all-gather.13.cloned.1.call-start = ((), (), s32[]{:S(2)}) async-start(), calls=%async_computation.10 | async-start | bytes 2359296 | tf_op jit(solution)/shard_map/all_gather | solution.py:769
  478.3 58.1 %copy-start.14 = (s32[2048]{0:T(1024)}, s32[2048]{0:T(1024)S(1)}, u32[]{:S(2)}) copy-start(s32[2048]{0:T(1024)S(1)} %get-tuple-element.70.refs_5_) | copy-start | bytes 24580
  495.5 41.0 %copy-start.10 = (s32[8192]{0:T(1024)}, s32[8192]{0:T(1024)S(1)}, u32[]{:S(2)}) copy-start(s32[8192]{0:T(1024)S(1)} %get-tuple-element.59.refs_2_) | copy-start | bytes 98308
  510.5 25.9 %copy-start.9 = (s32[8192]{0:T(1024)}, s32[8192]{0:T(1024)S(1)}, u32[]{:S(2)}) copy-start(s32[8192]{0:T(1024)S(1)} %get-tuple-element.69.refs_2_) | copy-start | bytes 98308
  526.8 9.7 %copy-start.2 = (f32[256,4096]{1,0:T(8,128)S(1)}, f32[256,4096]{1,0:T(8,128)}, u32[]{:S(2)}) copy-start(f32[256,4096]{1,0:T(8,128)} %get-tuple-element.66) | copy-start | bytes 12582916
  526.8 9.7 %copy-start.8 = (f32[256,1024]{1,0:T(8,128)S(1)}, f32[256,1024]{1,0:T(8,128)}, u32[]{:S(2)}) copy-start(f32[256,1024]{1,0:T(8,128)} %get-tuple-element.61.prevs) | copy-start | bytes 3145732
  720.6 3.5 copy-start.19
  (5 other events, 7.3 us)
Sparse Core Ops, SparseCore 0:
  160.0 95.0 all-gather.10
  308.3 71.3 reduce-scatter.2
  392.6 35.8 reduce-scatter.4
  443.2 54.4 all-gather.6
  499.5 56.4 all-gather.8
  557.7 37.1 all-gather.12
